TPU v7x, 256 devices: a whole 4x4x8 slice. The times are simulated.
256 devices in a mesh: segment: 2 (over x_lo), expert: 128 (over y, x_hi, z, core).
Axes of the slice: x: 4 (x_hi: 2, x_lo: 2; x = x_hi * 2 + x_lo), y: 4, z: 8, core: 2. Of those that a mesh axis runs over, the one named last changes fastest.
Arguments:
- boundary: bfloat16 [2, 8192, 2048], P('segment', 'expert'), may hold values from -6 to 6
- saved: bfloat16 [2, 8192, 2048], P('segment', 'expert'), may hold values from -6 to 6
- norm_gain: float32 [2, 2048], P('segment'), may hold values from 0.25 to 1.75
- gate_weight: bfloat16 [2, 128, 2048, 768], P('segment', 'expert'), may hold values from -0.125 to 0.125
- up_weight: bfloat16 [2, 128, 2048, 768], P('segment', 'expert'), may hold values from -0.125 to 0.125
- down_weight: bfloat16 [2, 128, 768, 2048], P('segment', 'expert'), may hold values from -0.21875 to 0.21875
- routes: int32 [2, 2, 8192, 8], P('segment', None, 'expert'), may hold values from 0 to 127, all different within a row; in each aligned block of 64 rows (0 to 63, 64 to 127, ..., all dimensions but the last counted through in order) at most 6 rows name the same one
- gate_codes: int32 [2, 2, 8192, 8], P('segment', None, 'expert'), may hold values from 1 to 16
Outputs:
- results: bfloat16 [2, 8192, 2048], P('segment', 'expert')
Inputs may be any that keep to these rules, and one draw needn't show every extreme that they name: `routes`: each row names 8 different experts. Among the rows of one index of expert (aligned blocks of 64 rows) no expert is named by more than 6 rows, a bound that some block reaches.
All inputs are finite; a program needn't handle non-finite values.
Results may differ from a plain program's by a relative error of at most 0.0075.
Values may be sent and summed in bfloat16 or wider, within the bound.
No kernel may reach another device: no remote copies, remote signals or barrier semaphores. Data moves between devices by JAX's collectives and lax.ppermute only.
A program may use at most 128 MiB of HBM per device.

v0:
```python
import jax
import jax.numpy as jnp
from jax import lax
from jax.sharding import Mesh
from jax.sharding import PartitionSpec as P

EXPERT = ("expert_0", "expert_1", "expert_2", "expert_3")


epsilon = 1e-06


def in_blocks(x, dim, length):
    before, after = (x.shape[:dim], x.shape[dim + 1 :])
    return jnp.moveaxis(x.reshape(*before, length, -1, *after), dim, 0)


def laid_out(parts, dim):
    shape = list(parts.shape[1:])
    shape[dim] *= parts.shape[0]
    return jnp.moveaxis(parts, 0, dim).reshape(shape)


def exchange_in_order(parts, axes, order):
    inside = parts.shape[1:]
    result = parts.reshape(*(lax.axis_size(a) for a in axes), *inside)
    for k in order:
        result = lax.all_to_all(result, axes[k], k, k, tiled=True)
    return result.reshape(-1, *inside)


def core_and_chips(x, groups, order, split_dim, concat_dim):
    length = lax.axis_size(groups[0]) * lax.axis_size(groups[1])
    parts = in_blocks(x, split_dim, length)
    return laid_out(exchange_in_order(parts, groups, order), concat_dim)


def from_partner(block, axis, stride):
    count = lax.axis_size(axis)
    route = []
    for low in range(count):
        high = low | 1 << stride
        if high != low and high < count:
            route += [(low, high), (high, low)]
    return lax.ppermute(block, axis, route)


def gate_values(codes):
    counted = codes.astype(jnp.float32)
    return counted / jnp.sum(counted, axis=-1, keepdims=True)


def normalize(inputs, gain_row):
    widened = inputs.astype(jnp.float32)
    scaling = lax.rsqrt(jnp.mean(widened * widened, axis=-1, keepdims=True) + epsilon)
    return (widened, scaling, (widened * scaling * gain_row).astype(jnp.bfloat16))


def transposed(left, right):
    return lax.dot_general(
        left, right, (((1,), (1,)), ((), ())), preferred_element_type=jnp.float32
    )


def expert_forward(row_block, w_gate, w_up, w_down):
    gate_part = jnp.dot(row_block, w_gate, preferred_element_type=jnp.float32)
    up_part = jnp.dot(row_block, w_up, preferred_element_type=jnp.float32)
    hidden = (gate_part * jax.nn.sigmoid(gate_part) * up_part).astype(jnp.bfloat16)
    return jnp.dot(hidden, w_down, preferred_element_type=jnp.float32).astype(jnp.bfloat16)


def expert_backward(row_block, grad_block, w_gate, w_up, w_down):
    gate_part = jnp.dot(row_block, w_gate, preferred_element_type=jnp.float32)
    up_part = jnp.dot(row_block, w_up, preferred_element_type=jnp.float32)
    sigmoid_part = jax.nn.sigmoid(gate_part)
    activated = gate_part * sigmoid_part
    slope = sigmoid_part * (1.0 + gate_part * (1.0 - sigmoid_part))
    hidden_grad = transposed(grad_block, w_down)
    gate_grad = (hidden_grad * up_part * slope).astype(jnp.bfloat16)
    up_grad = (hidden_grad * activated).astype(jnp.bfloat16)
    return (transposed(gate_grad, w_gate) + transposed(up_grad, w_up)).astype(jnp.bfloat16)


def layout(route, codes, n_peer, capacity):
    tokens, top_count = route.shape
    flat_ids = route.reshape(-1)
    onehot = (flat_ids[:, None] == jnp.arange(n_peer, dtype=jnp.int32)[None, :]).astype(jnp.int32)
    rank_in = jnp.sum(jnp.cumsum(onehot, axis=0) * onehot, axis=1) - 1
    slot_of = flat_ids * capacity + rank_in
    slot_ids = jnp.arange(n_peer * capacity, dtype=jnp.int32)
    slot_hit = (slot_ids[:, None, None] == slot_of.reshape(tokens, top_count)[None, :, :]).astype(
        jnp.bfloat16
    )
    placing = jnp.sum(slot_hit, axis=2, dtype=jnp.float32).astype(jnp.bfloat16)
    return (placing, slot_of, gate_values(codes))


def dispatch(placing, payload, n_peer, capacity):
    picked = jnp.dot(placing, payload, preferred_element_type=jnp.float32).astype(jnp.bfloat16)
    return picked.reshape(n_peer, capacity, payload.shape[-1])


def collect(slot_of, gates, came_back):
    flat_rows = came_back.reshape(-1, came_back.shape[-1])
    chosen = jnp.take(flat_rows, slot_of, axis=0).reshape(
        gates.shape[0], gates.shape[1], flat_rows.shape[-1]
    )
    return jnp.einsum("tk,tkd->td", gates, chosen.astype(jnp.float32))


def apply_expert(forward_flag, first_rows, second_rows, weights):
    layout_of = first_rows.shape
    row_block = first_rows.reshape(-1, layout_of[-1])
    grad_block = second_rows.reshape(-1, layout_of[-1])
    outcome = lax.cond(
        forward_flag,
        lambda: expert_forward(row_block, weights[0], weights[1], weights[2]),
        lambda: expert_backward(row_block, grad_block, weights[0], weights[1], weights[2]),
    )
    return outcome.reshape(layout_of)


def return_rows(outcome):
    return core_and_chips(outcome, (("expert_0", "expert_1", "expert_2"), "expert_3"), (1, 0), 0, 0)


def finish(widened, scaling, gain_row, upstream, summed, forward_flag):
    forward_out = widened + summed
    scaled = summed * gain_row
    inner_mean = jnp.mean(scaled * widened, axis=-1, keepdims=True)
    cubed = scaling * scaling * scaling
    backward_out = upstream.astype(jnp.float32) + scaling * scaled - widened * cubed * inner_mean
    return jnp.where(forward_flag, forward_out, backward_out).astype(jnp.bfloat16)


def body(boundary, saved, norm_gain, gate_weight, up_weight, down_weight, routes, gate_codes):
    first_segment = lax.axis_index("segment") == 0
    later_forward = jnp.logical_not(first_segment)
    n_peer = lax.axis_size(EXPERT)
    tokens = boundary.shape[1]
    top_count = routes.shape[3]
    capacity = max(2, 3 * tokens * top_count // (2 * n_peer))
    weights = (gate_weight[0, 0], up_weight[0, 0], down_weight[0, 0])
    gain_row = norm_gain[0]
    edge_rows = boundary[0]
    stored = saved[0]
    route_now = jnp.where(first_segment, routes[0, 0], routes[0, 1])
    codes_now = jnp.where(first_segment, gate_codes[0, 0], gate_codes[0, 1])
    route_next = jnp.where(first_segment, routes[0, 1], routes[0, 0])
    codes_next = jnp.where(first_segment, gate_codes[0, 1], gate_codes[0, 0])
    place_now, slots_now, gates_now = layout(route_now, codes_now, n_peer, capacity)
    place_next, slots_next, gates_next = layout(route_next, codes_next, n_peer, capacity)
    inputs_now = jnp.where(first_segment, edge_rows, stored)
    widened, scaling, normed = normalize(inputs_now, gain_row)
    stored_normed = normalize(stored, gain_row)[2]
    early_rows = jnp.where(first_segment, stored_normed, edge_rows)
    early_place = jnp.where(first_segment, place_next, place_now)
    outgoing = (
        dispatch(place_now, normed, n_peer, capacity),
        dispatch(early_place, early_rows, n_peer, capacity),
    )
    paired = (
        lax.all_to_all(outgoing[0], EXPERT, split_axis=0, concat_axis=0, tiled=True),
        lax.all_to_all(outgoing[1], EXPERT, split_axis=0, concat_axis=0, tiled=True),
    )
    outcome = apply_expert(first_segment, paired[0], paired[1], weights)
    came_back = return_rows(outcome)
    kept_rows = paired[1]
    produced = finish(
        widened,
        scaling,
        gain_row,
        edge_rows,
        collect(slots_now, gates_now, came_back),
        first_segment,
    )
    arrived = from_partner(produced, "segment", 0)
    inputs_next = jnp.where(first_segment, stored, arrived)
    widened_next, scaling_next, normed_next = normalize(inputs_next, gain_row)
    member = jnp.where(first_segment, arrived, normed_next)
    landed = lax.all_to_all(
        dispatch(place_next, member, n_peer, capacity),
        EXPERT,
        split_axis=0,
        concat_axis=0,
        tiled=True,
    )
    outcome = apply_expert(
        later_forward, jnp.where(first_segment, kept_rows, landed), landed, weights
    )
    came_next = return_rows(outcome)
    result = finish(
        widened_next,
        scaling_next,
        gain_row,
        arrived,
        collect(slots_next, gates_next, came_next),
        later_forward,
    )
    return result[None]


def solution(mesh):
    finer = Mesh(
        mesh.devices.reshape(mesh.shape["segment"], 4, 2, 8, 2),
        ("segment", "expert_0", "expert_1", "expert_2", "expert_3"),
    )
    placed = (
        P("segment", EXPERT, None),
        P("segment", EXPERT, None),
        P("segment", None),
        P("segment", EXPERT, None, None),
        P("segment", EXPERT, None, None),
        P("segment", EXPERT, None, None),
        P("segment", None, EXPERT, None),
        P("segment", None, EXPERT, None),
    )
    return jax.shard_map(
        body, mesh=finer, in_specs=placed, out_specs=P("segment", EXPERT, None), check_vma=False
    )
```

profile of v0, /device:TPU:96, one launch (start us, length us, event | category | flops | bytes accessed | tf_op | source)
XLA Modules:
  0.0 674.3 jit_solution(996519767387054084)
XLA Ops:
  0.0 0.8 fusion.73
  1.4 0.2 fusion.62
  1.8 0.2 fusion.50
  2.2 0.2 fusion.60
  2.5 0.2 fusion.51
  2.8 0.6 copy-done.12
  3.5 0.5 fusion.24
  4.0 0.7 fusion.29
  4.8 0.6 multiply_multiply_fusion.1
  5.5 0.5 copy-done.15
  5.9 1.0 convolution_convert_fusion.1
  7.0 2.9 reshape.201
  9.8 14.7 %all-to-all-start.1 = ((bf16[128,6,2048]{2,1,0:T(8,128)(2,1)}), bf16[128,6,2048]{2,1,0:T(8,128)(2,1)}, u32[]{:S(2)}, u32[]{:S(2)}) async-start(bf16[128,6,2048]{2,1,0:T(8,128)(2,1)} %reshape.201), calls=%async_computation.1 | async-start | bytes 8388608 | tf_op jit(solution)/shard_map/all_to_all | solution.py:163
  24.5 0.5 fusion.25
  25.1 0.6 copy-done.7
  25.7 2.0 convolution_convert_fusion.2
  27.7 2.8 reshape.200
  30.6 91.8 %all-to-all-done.1 = bf16[128,6,2048]{2,1,0:T(8,128)(2,1)} async-done(((bf16[128,6,2048]{2,1,0:T(8,128)(2,1)}), bf16[128,6,2048]{2,1,0:T(8,128)(2,1)}, u32[]{:S(2)}, u32[]{:S(2)}) %all-to-all-start.1) | async-done | bytes 3145760 | tf_op jit(solution)/shard_map/all_to_all | solution.py:163
  122.4 7.3 %all-to-all-start = ((bf16[128,6,2048]{2,1,0:T(8,128)(2,1)}), bf16[128,6,2048]{2,1,0:T(8,128)(2,1)}, u32[]{:S(2)}, u32[]{:S(2)}) async-start(bf16[128,6,2048]{2,1,0:T(8,128)(2,1)} %reshape.200), calls=%async_computation | async-start | bytes 8388608 | tf_op jit(solution)/shard_map/all_to_all | solution.py:164
  129.7 4.9 reshape.202
  134.6 93.0 %all-to-all-done = bf16[128,6,2048]{2,1,0:T(8,128)(2,1)} async-done(((bf16[128,6,2048]{2,1,0:T(8,128)(2,1)}), bf16[128,6,2048]{2,1,0:T(8,128)(2,1)}, u32[]{:S(2)}, u32[]{:S(2)}) %all-to-all-start) | async-done | bytes 3145760 | tf_op jit(solution)/shard_map/all_to_all | solution.py:164
  227.5 25.9 %conditional.4 = (bf16[768,2048]{1,0:T(8,128)(2,1)}) conditional(s32[]{:T(128)} %convert_element_type.110, (bf16[128,6,2048]{2,1,0:T(8,128)(2,1)}, bf16[768,2048]{1,0:T(8,128)(2,1)}, bf16[768,2048]{1,0:T(8,128)(2,1)S(1)}, bf16[2048,768]{1,0:T(8,128)(2,1)}, bf16[2048,768]{1,0:T(8,128)(2,1)}) %tuple.52, (bf16[768,2048]{1,0:T(8,128)(2,1)S(1)}, ...), branch_computations={%region_11.12_spmd, %region_12.13_spmd} | conditional | flops 12092178432 | bytes 61341704
  236.5 5.9 fusion.77
  242.4 11.1 %fusion.4 = bf16[768,2048]{1,0:T(8,128)(2,1)} fusion(bf16[768,2048]{1,0:T(8,128)(2,1)} %get-tuple-element.62, f32[768,768]{1,0:T(8,128)} %fusion.77, bf16[768,2048]{1,0:T(8,128)(2,1)S(1)} %get-tuple-element.59, bf16[2048,768]{1,0:T(8,128)(2,1)} %get-tuple-element.61), kind=kOutput, calls=%fused_computation.11 | convolution fusion | flops 4835377152 | bytes 14942208 | tf_op jit(solution)/shard_map/cond/branch_1_fun/dot_general | solution.py:69
  253.4 6.2 reshape_reshape_reshape.12
  259.7 3.9 copy.41
  263.6 6.3 all_to_all.35
  269.9 4.9 copy.42
  274.8 6.4 all-to-all-start.3
  281.4 0.5 compare_and_fusion.1
  282.1 73.2 %all-to-all-done.3 = bf16[64,2,1,6,2048]{4,1,3,2,0:T(2,128)(2,1)S(1)} async-done(((bf16[64,2,1,6,2048]{4,1,3,2,0:T(2,128)(2,1)}), bf16[64,2,1,6,2048]{4,1,3,2,0:T(2,128)(2,1)S(1)}, u32[]{:S(2)}, u32[]{:S(2)}) %all-to-all-start.3) | async-done | bytes 3145760 | tf_op jit(solution)/shard_map/all_to_all | solution.py:28
  355.3 3.6 copy.43
  358.9 4.9 reshape_reshape_reshape.13
  363.8 3.3 gather_fusion
  367.1 2.4 fusion.14
  369.6 0.3 fusion.36
  369.9 0.3 fusion.33
  370.2 16.7 %collective-permute-start = (bf16[64,2048]{1,0:T(8,128)(2,1)S(1)}, bf16[64,2048]{1,0:T(8,128)(2,1)S(1)}, u32[]{:S(2)}, u32[]{:S(2)}) collective-permute-start(bf16[64,2048]{1,0:T(8,128)(2,1)S(1)} %fusion.33), channel_id=1, source_target_pairs={{0,128},{128,0},{1,129},{129,1},{2,130},{130,2},{3,131},{131,3},{4... | collective-permute-start | bytes 786440 | tf_op jit(solution)/shard_map/ppermute | solution.py:45
  386.9 4.4 collective-permute-done
  391.5 0.5 copy-done.1
  392.0 1.1 convolution_convert_fusion
  393.0 2.9 reshape.204
  395.9 11.5 %all-to-all-start.4 = ((bf16[128,6,2048]{2,1,0:T(8,128)(2,1)}), bf16[128,6,2048]{2,1,0:T(8,128)(2,1)}, u32[]{:S(2)}, u32[]{:S(2)}) async-start(bf16[128,6,2048]{2,1,0:T(8,128)(2,1)} %reshape.204), calls=%async_computation.4 | async-start | bytes 8388608 | tf_op jit(solution)/shard_map/all_to_all | solution.py:181
  407.4 97.8 %all-to-all-done.4 = bf16[128,6,2048]{2,1,0:T(8,128)(2,1)} async-done(((bf16[128,6,2048]{2,1,0:T(8,128)(2,1)}), bf16[128,6,2048]{2,1,0:T(8,128)(2,1)}, u32[]{:S(2)}, u32[]{:S(2)}) %all-to-all-start.4) | async-done | bytes 3145760 | tf_op jit(solution)/shard_map/all_to_all | solution.py:181
  505.2 4.6 broadcast_select_fusion
  509.8 4.9 reshape.205
  514.7 41.8 %conditional.5 = (bf16[768,2048]{1,0:T(8,128)(2,1)}) conditional(s32[]{:T(128)} %convert_element_type.126, (bf16[128,6,2048]{2,1,0:T(8,128)(2,1)}, bf16[768,2048]{1,0:T(8,128)(2,1)}, bf16[768,2048]{1,0:T(8,128)(2,1)S(1)}, bf16[2048,768]{1,0:T(8,128)(2,1)}, bf16[2048,768]{1,0:T(8,128)(2,1)}) %tuple.54, (bf16[768,2048]{1,0:T(8,128)(2,1)S(1)}, ...), branch_computations={%region_16.18_spmd, %region_17.19_spmd} | conditional | flops 12092178432 | bytes 61341704
  515.1 5.9 fusion.79
  521.0 6.3 reshape.188
  527.3 6.9 %fusion.78 = f32[768,768]{1,0:T(8,128)} fusion(bf16[768,2048]{1,0:T(8,128)(2,1)} %reshape.188, bf16[768,2048]{1,0:T(8,128)(2,1)} %get-tuple-element.64), kind=kOutput, calls=%fused_computation.144 | convolution fusion | flops 2415919104 | bytes 8650752 | tf_op jit(solution)/shard_map/cond/branch_0_fun/dot_general | solution.py:60
  534.2 12.7 %fusion.7 = f32[768,2048]{1,0:T(8,128)} fusion(bf16[2048,768]{1,0:T(8,128)(2,1)} %get-tuple-element.67, f32[768,768]{1,0:T(8,128)} %fusion.79, f32[768,768]{1,0:T(8,128)} %fusion.78, bf16[768,2048]{1,0:T(8,128)(2,1)S(1)} %get-tuple-element.65, bf16[2048,768]{1,0:T(8,128)(2,1)} %get-tuple-element.66), kind=kOutput, calls=%fused_computation.18 | convolution fusion | flops 4837736448 | bytes 20447232 | tf_op jit(solution)/shard_map/cond/branch_0_fun/dot_general | solution.py:60
  546.9 9.5 %convolution_add_fusion.1 = bf16[768,2048]{1,0:T(8,128)(2,1)} fusion(f32[768,2048]{1,0:T(8,128)} %fusion.7, bf16[2048,768]{1,0:T(8,128)(2,1)} %get-tuple-element.66, f32[768,768]{1,0:T(8,128)} %fusion.78, f32[768,768]{1,0:T(8,128)} %fusion.79), kind=kOutput, calls=%fused_computation.13 | convolution fusion | flops 2422603776 | bytes 17301504 | tf_op jit(solution)/shard_map/cond/branch_0_fun/dot_general | solution.py:60
  556.5 6.3 reshape_reshape_reshape.14
  562.8 3.9 copy.44
  566.7 6.3 all_to_all.36
  573.0 4.9 copy.45
  577.9 6.4 all-to-all-start.6
  584.3 74.1 %all-to-all-done.6 = bf16[64,2,1,6,2048]{4,1,3,2,0:T(2,128)(2,1)S(1)} async-done(((bf16[64,2,1,6,2048]{4,1,3,2,0:T(2,128)(2,1)}), bf16[64,2,1,6,2048]{4,1,3,2,0:T(2,128)(2,1)S(1)}, u32[]{:S(2)}, u32[]{:S(2)}) %all-to-all-start.6) | async-done | bytes 3145760 | tf_op jit(solution)/shard_map/all_to_all | solution.py:28
  658.4 3.6 copy.46
  662.0 4.9 reshape_reshape_reshape.15
  666.9 3.3 gather_fusion.1
  670.2 2.4 fusion.12
  672.6 0.3 fusion.44
  672.9 1.2 fusion.66
  (75 shorter events, 1.9 us)
Async XLA Ops:
  0.0 4.0 copy-start.5
  0.0 4.0 copy-start
  0.0 5.9 copy-start.9
  2.0 0.8 copy-start.10
  2.8 0.6 copy-start.12
  4.8 0.7 copy-start.3
  5.4 0.5 copy-start.15
  9.8 15.2 %copy-start.19 = (f32[64]{0:T(128)S(1)}, f32[64]{0:T(128)}, u32[]{:S(2)}) copy-start(f32[64]{0:T(128)} %get-tuple-element.80) | copy-start | bytes 772
  9.8 112.5 %all-to-all-start.1 = ((bf16[128,6,2048]{2,1,0:T(8,128)(2,1)}), bf16[128,6,2048]{2,1,0:T(8,128)(2,1)}, u32[]{:S(2)}, u32[]{:S(2)}) async-start(bf16[128,6,2048]{2,1,0:T(8,128)(2,1)} %reshape.201), calls=%async_computation.1 | async-start | bytes 8388608 | tf_op jit(solution)/shard_map/all_to_all | solution.py:163
  25.1 0.6 copy-start.7
  122.4 105.1 %all-to-all-start = ((bf16[128,6,2048]{2,1,0:T(8,128)(2,1)}), bf16[128,6,2048]{2,1,0:T(8,128)(2,1)}, u32[]{:S(2)}, u32[]{:S(2)}) async-start(bf16[128,6,2048]{2,1,0:T(8,128)(2,1)} %reshape.200), calls=%async_computation | async-start | bytes 8388608 | tf_op jit(solution)/shard_map/all_to_all | solution.py:164
  274.8 6.4 copy-start.14
  274.8 6.6 copy-start.13
  274.8 80.5 %all-to-all-start.3 = ((bf16[64,2,1,6,2048]{4,1,3,2,0:T(2,128)(2,1)}), bf16[64,2,1,6,2048]{4,1,3,2,0:T(2,128)(2,1)S(1)}, u32[]{:S(2)}, u32[]{:S(2)}) async-start(bf16[64,2,1,6,2048]{4,1,3,2,0:T(2,128)(2,1)} %copy.42), calls=%async_computation.3 | async-start | bytes 6291456 | tf_op jit(solution)/shard_map/all_to_all | solution.py:28
  363.7 3.4 copy-start.18
  367.1 2.5 copy-start.4
  367.1 2.8 copy-start.6
  367.1 2.8 copy-start.16
  367.1 2.8 copy-start.17
  367.1 24.9 %copy-start.8 = (bf16[768,64]{0,1:T(8,128)(2,1)S(1)}, bf16[768,64]{0,1:T(8,128)(2,1)}, u32[]{:S(2)}) copy-start(bf16[768,64]{0,1:T(8,128)(2,1)} %copy-done.7) | copy-start | bytes 294916
  370.2 21.0 %collective-permute-start = (bf16[64,2048]{1,0:T(8,128)(2,1)S(1)}, bf16[64,2048]{1,0:T(8,128)(2,1)S(1)}, u32[]{:S(2)}, u32[]{:S(2)}) collective-permute-start(bf16[64,2048]{1,0:T(8,128)(2,1)S(1)} %fusion.33), channel_id=1, source_target_pairs={{0,128},{128,0},{1,129},{129,1},{2,130},{130,2},{3,131},{131,3},{4... | collective-permute-start | bytes 786440 | tf_op jit(solution)/shard_map/ppermute | solution.py:45
  391.3 0.7 copy-start.1
  395.9 109.4 %all-to-all-start.4 = ((bf16[128,6,2048]{2,1,0:T(8,128)(2,1)}), bf16[128,6,2048]{2,1,0:T(8,128)(2,1)}, u32[]{:S(2)}, u32[]{:S(2)}) async-start(bf16[128,6,2048]{2,1,0:T(8,128)(2,1)} %reshape.204), calls=%async_computation.4 | async-start | bytes 8388608 | tf_op jit(solution)/shard_map/all_to_all | solution.py:181
  577.9 6.4 copy-start.11
  577.9 80.5 %all-to-all-start.6 = ((bf16[64,2,1,6,2048]{4,1,3,2,0:T(2,128)(2,1)}), bf16[64,2,1,6,2048]{4,1,3,2,0:T(2,128)(2,1)S(1)}, u32[]{:S(2)}, u32[]{:S(2)}) async-start(bf16[64,2,1,6,2048]{4,1,3,2,0:T(2,128)(2,1)} %copy.45), calls=%async_computation.6 | async-start | bytes 6291456 | tf_op jit(solution)/shard_map/all_to_all | solution.py:28
  670.2 2.4 copy-start.2
where the time goes:
time: 685 us; the launch traced here: 674 us
  waiting for transfers between devices  434 us (63%)
  local copies, waits for them, and re-layouts  82.5 us (12%)
  starting transfers between devices  62.9 us (9%)
  matrix products  60.8 us (9%)
  blocking collectives  12.5 us (2%)
  other arithmetic  11.1 us (2%)
  loops' own time  9.52 us (1%)
    all_to_all x2, waiting for transfers between devices, exchange_in_order(): result = lax.all_to_all(result, axes[k], k, k, tiled=True)  147 us
    all_to_all x1, waiting for transfers between devices, body(): lax.all_to_all(dispatch(place_next, member, n_peer, capacity), EXPERT, sp...  97.8 us
    all_to_all x1, waiting for transfers between devices, body(): lax.all_to_all(outgoing[1], EXPERT, split_axis=0, concat_axis=0, tiled=True)  93 us
    all_to_all x1, waiting for transfers between devices, body(): lax.all_to_all(outgoing[0], EXPERT, split_axis=0, concat_axis=0, tiled=True)  91.8 us
    dot_general x3, matrix products, transposed(): lax.dot_general(left, right, (((1,), (1,)), ((), ())), preferred_element_...  29.1 us
    another operation x4, local copies, waits for them, and re-layouts, exchange_in_order(): result = parts.reshape(*(lax.axis_size(a) for a in axes), *inside)  20.3 us
    all_to_all x4, local copies, waits for them, and re-layouts, exchange_in_order(): result = lax.all_to_all(result, axes[k], k, k, tiled=True)  17 us
    ppermute x1, starting transfers between devices, from_partner(): return lax.ppermute(block, axis, route)  16.7 us
  transfers between devices with their start and end apart: 6, of which 6 were waited for; matrix products, arithmetic and copies ran while one was open for 2% of the time, Pallas kernels for 0%

commit v1 on v0

v1 whole, which is shorter than its diff:
```python
import jax
import jax.numpy as jnp
from jax import lax
from jax.sharding import Mesh
from jax.sharding import PartitionSpec as P

EXPERT = ("expert_0", "expert_1", "expert_2", "expert_3")
PLANE = ("expert_0", "expert_1", "expert_3")
RING = "expert_2"

CHUNKS = ((0, -1, 1, -2), (2, -3, 3, 4))
CAPACITY = 6

epsilon = 1e-06


def step_ring(block, step):
    count = lax.axis_size(RING)
    return lax.ppermute(block, RING, [(i, (i + step) % count) for i in range(count)])


def gather_ring(own):
    half = own.shape[0] // 2
    blocks = {0: own}
    for distance in (1, 2, 3):
        blocks[-distance] = step_ring(blocks[1 - distance], 1)
        blocks[distance] = step_ring(blocks[distance - 1], -1)
    blocks[4] = jnp.concatenate(
        (step_ring(blocks[-3][:half], 1), step_ring(blocks[3][half:], -1)), axis=0
    )
    return blocks


def sum_ring(parts):
    half = parts[4].shape[0] // 2
    up = step_ring(parts[4][:half].astype(jnp.bfloat16), 1).astype(jnp.float32)
    down = step_ring(parts[4][half:].astype(jnp.bfloat16), -1).astype(jnp.float32)
    up = jnp.concatenate((parts[3][:half] + up, parts[3][half:]), axis=0)
    down = jnp.concatenate((parts[-3][:half], parts[-3][half:] + down), axis=0)
    for distance in (2, 1):
        up = parts[distance] + step_ring(up.astype(jnp.bfloat16), 1).astype(jnp.float32)
        down = parts[-distance] + step_ring(down.astype(jnp.bfloat16), -1).astype(jnp.float32)
    up = step_ring(up.astype(jnp.bfloat16), 1).astype(jnp.float32)
    down = step_ring(down.astype(jnp.bfloat16), -1).astype(jnp.float32)
    return parts[0] + up + down


def exchange(rows):
    count = lax.axis_size(PLANE)
    parts = rows.reshape(count, -1, rows.shape[-1])
    moved = lax.all_to_all(parts, PLANE, split_axis=0, concat_axis=0, tiled=True)
    return moved.reshape(rows.shape)


def slots(ids, codes):
    width = ids.shape[1]
    tokens = 64
    blocks = width // tokens
    peers = lax.axis_size(PLANE)
    plane = lax.broadcasted_iota(jnp.int32, (peers, 1, 1), 0)
    named = ((plane // 2) * lax.axis_size(RING) + lax.axis_index(RING)) * 2 + plane % 2
    hit = ids[None] == named.astype(jnp.float32)
    member = jnp.sum(hit.astype(jnp.float32), axis=1)
    code = jnp.sum(jnp.where(hit, codes[None], 0.0), axis=1)
    row = lax.broadcasted_iota(jnp.int32, (width, width), 0)
    column = lax.broadcasted_iota(jnp.int32, (width, width), 1)
    earlier = ((row // tokens == column // tokens) & (row < column)).astype(jnp.bfloat16)
    rank = jnp.dot(member.astype(jnp.bfloat16), earlier, preferred_element_type=jnp.float32)
    block = lax.broadcasted_iota(jnp.int32, (1, width), 1) // tokens
    key = jnp.where(member > 0.0, (block * CAPACITY).astype(jnp.float32) + rank, -1.0)
    place = lax.broadcasted_iota(jnp.int32, (1, blocks * CAPACITY, 1), 1).astype(jnp.float32)
    found = key[:, None, :] == place
    picking = found.astype(jnp.bfloat16)
    weighing = jnp.where(found, code[:, None, :], 0.0).astype(jnp.bfloat16)
    return (picking.reshape(-1, width), weighing.reshape(-1, width))


def pick(picking, tokens):
    return jnp.dot(picking, tokens, preferred_element_type=jnp.float32).astype(jnp.bfloat16)


def combine(weighing, rows):
    return lax.dot_general(
        weighing, rows, (((0,), (0,)), ((), ())), preferred_element_type=jnp.float32
    )


def normalize(inputs, gain_row):
    widened = inputs.astype(jnp.float32)
    scaling = lax.rsqrt(jnp.mean(widened * widened, axis=-1, keepdims=True) + epsilon)
    return (widened, scaling, (widened * scaling * gain_row).astype(jnp.bfloat16))


def transposed(left, right):
    return lax.dot_general(
        left, right, (((1,), (1,)), ((), ())), preferred_element_type=jnp.float32
    )


def expert_forward(row_block, w_gate, w_up, w_down):
    gate_part = jnp.dot(row_block, w_gate, preferred_element_type=jnp.float32)
    up_part = jnp.dot(row_block, w_up, preferred_element_type=jnp.float32)
    hidden = (gate_part * jax.nn.sigmoid(gate_part) * up_part).astype(jnp.bfloat16)
    return jnp.dot(hidden, w_down, preferred_element_type=jnp.float32).astype(jnp.bfloat16)


def expert_backward(row_block, grad_block, w_gate, w_up, w_down):
    gate_part = jnp.dot(row_block, w_gate, preferred_element_type=jnp.float32)
    up_part = jnp.dot(row_block, w_up, preferred_element_type=jnp.float32)
    sigmoid_part = jax.nn.sigmoid(gate_part)
    activated = gate_part * sigmoid_part
    slope = sigmoid_part * (1.0 + gate_part * (1.0 - sigmoid_part))
    hidden_grad = transposed(grad_block, w_down)
    gate_grad = (hidden_grad * up_part * slope).astype(jnp.bfloat16)
    up_grad = (hidden_grad * activated).astype(jnp.bfloat16)
    return (transposed(gate_grad, w_gate) + transposed(up_grad, w_up)).astype(jnp.bfloat16)


def apply_expert(forward_flag, rows, grads, weights):
    return lax.cond(
        forward_flag,
        lambda: expert_forward(rows, *weights),
        lambda: expert_backward(rows, grads, *weights),
    )


def finish(widened, scaling, gain_row, upstream, summed, forward_flag):
    forward_out = widened + summed
    scaled = summed * gain_row
    inner_mean = jnp.mean(scaled * widened, axis=-1, keepdims=True)
    cubed = scaling * scaling * scaling
    backward_out = upstream.astype(jnp.float32) + scaling * scaled - widened * cubed * inner_mean
    return jnp.where(forward_flag, forward_out, backward_out).astype(jnp.bfloat16)


def stack(blocks, chunk):
    return jnp.concatenate([blocks[k] for k in chunk], axis=0)


def returned(outcomes, weighings, code_sum):
    parts = {}
    for chunk, outcome, weighing in reversed(list(zip(CHUNKS, outcomes, weighings))):
        share = combine(weighing, exchange(outcome)).reshape(len(chunk), -1, outcome.shape[-1])
        for i, k in enumerate(chunk):
            parts[k] = share[i]
    return sum_ring(parts) / code_sum


def body(boundary, saved, norm_gain, gate_weight, up_weight, down_weight, routes, gate_codes):
    first_segment = lax.axis_index("segment") == 0
    later_forward = jnp.logical_not(first_segment)
    width = boundary.shape[2]
    weights = (gate_weight[0, 0], up_weight[0, 0], down_weight[0, 0])
    gain_row = norm_gain[0]
    edge_rows = boundary[0]
    stored = saved[0]
    route_now = jnp.where(first_segment, routes[0, 0], routes[0, 1])
    codes_now = jnp.where(first_segment, gate_codes[0, 0], gate_codes[0, 1])
    route_next = jnp.where(first_segment, routes[0, 1], routes[0, 0])
    codes_next = jnp.where(first_segment, gate_codes[0, 1], gate_codes[0, 0])
    sum_now = jnp.sum(codes_now.astype(jnp.float32), axis=-1, keepdims=True)
    sum_next = jnp.sum(codes_next.astype(jnp.float32), axis=-1, keepdims=True)
    top = route_now.shape[1]
    info = jnp.concatenate((route_now, codes_now, route_next, codes_next), axis=1)
    info = jnp.pad(info.astype(jnp.bfloat16), ((0, 0), (0, 128 - 4 * top)))

    inputs_now = jnp.where(first_segment, edge_rows, stored)
    widened, scaling, normed = normalize(inputs_now, gain_row)
    stored_normed = normalize(stored, gain_row)[2]
    early_rows = jnp.where(first_segment, stored_normed, edge_rows)

    blocks = gather_ring(jnp.concatenate((normed, info), axis=1))
    early_blocks = gather_ring(early_rows)
    arrived_rows, kept_rows, place_next, weigh_now, weigh_next = [], [], [], [], []
    for chunk in CHUNKS:
        tokens = stack(blocks, chunk)
        told = jnp.transpose(tokens[:, width : width + 4 * top]).astype(jnp.float32)
        pick_now, by_now = slots(told[:top], told[top : 2 * top])
        pick_next, by_next = slots(told[2 * top : 3 * top], told[3 * top :])
        pick_early = jnp.where(first_segment, pick_next, pick_now)
        arrived_rows.append(exchange(pick(pick_now, tokens[:, :width])))
        kept_rows.append(exchange(pick(pick_early, stack(early_blocks, chunk))))
        place_next.append(pick_next)
        weigh_now.append(by_now)
        weigh_next.append(by_next)
    outcomes = [
        apply_expert(first_segment, rows, grads, weights)
        for rows, grads in zip(arrived_rows, kept_rows)
    ]
    summed = returned(outcomes, weigh_now, sum_now)
    produced = finish(widened, scaling, gain_row, edge_rows, summed, first_segment)

    arrived = lax.ppermute(produced, "segment", [(0, 1), (1, 0)])
    inputs_next = jnp.where(first_segment, stored, arrived)
    widened_next, scaling_next, normed_next = normalize(inputs_next, gain_row)
    member_blocks = gather_ring(jnp.where(first_segment, arrived, normed_next))
    outcomes = []
    for i, chunk in enumerate(CHUNKS):
        landed = exchange(pick(place_next[i], stack(member_blocks, chunk)))
        rows = jnp.where(first_segment, kept_rows[i], landed)
        outcomes.append(apply_expert(later_forward, rows, landed, weights))
    summed = returned(outcomes, weigh_next, sum_next)
    result = finish(widened_next, scaling_next, gain_row, arrived, summed, later_forward)
    return result[None]


def solution(mesh):
    finer = Mesh(
        mesh.devices.reshape(mesh.shape["segment"], 4, 2, 8, 2),
        ("segment", "expert_0", "expert_1", "expert_2", "expert_3"),
    )
    placed = (
        P("segment", EXPERT, None),
        P("segment", EXPERT, None),
        P("segment", None),
        P("segment", EXPERT, None, None),
        P("segment", EXPERT, None, None),
        P("segment", EXPERT, None, None),
        P("segment", None, EXPERT, None),
        P("segment", None, EXPERT, None),
    )
    return jax.shard_map(
        body, mesh=finer, in_specs=placed, out_specs=P("segment", EXPERT, None), check_vma=False
    )
```

time: 685 us -> 508 us (0.74)
  waiting for transfers between devices: 434 us -> 254 us
  local copies, waits for them, and re-layouts: 82.5 us -> 13.2 us
  starting transfers between devices: 62.9 us -> 111 us
  matrix products: 60.8 us -> 95.3 us
  blocking collectives: 12.5 us -> 0 us
  other arithmetic: 11.1 us -> 21.6 us
  loops' own time: 9.52 us -> 1.04 us
    all_to_all x5 -> x10, waiting for transfers between devices: 430 us -> 174 us  [exchange(): lax.all_to_all(parts, PLANE, split_axis=0, concat_axis=0, tiled=True)]
    ppermute x1 -> x41, waiting for transfers between devices: 4.35 us -> 80 us  [the longest x40 75.7 us: step_ring(): lax.ppermute(block, RING, [(i, (i + step) % count) for i in range(count)])]
    ppermute x1 -> x41, starting transfers between devices: 16.7 us -> 68 us  [the longest x40 55.8 us: step_ring(): lax.ppermute(block, RING, [(i, (i + step) % count) for i in range(count)])]
    another operation x12 -> x10, local copies, waits for them, and re-layouts: 30.1 us -> 0.02 us  [the longest x4 20.3 us: exchange_in_order(): result = parts.reshape(*(lax.axis_size(a) for a in axes), *inside)]
    reshape x6 -> x0, local copies, waits for them, and re-layouts: 24.6 us -> none  [the longest x2 9.75 us: apply_expert(): row_block = first_rows.reshape(-1, layout_of[-1])]
    dot_general x5 -> x14, matrix products: 8.93 us -> 26.1 us  [the longest x6 14.1 us: pick(): jnp.dot(picking, tokens, preferred_element_type=jnp.float32)]
    all_to_all x4 -> x0, local copies, waits for them, and re-layouts: 17 us -> none  [exchange_in_order(): result = lax.all_to_all(result, axes[k], k, k, tiled=True)]
    all_to_all x2 -> x0, blocking collectives: 12.5 us -> none  [exchange_in_order(): result = lax.all_to_all(result, axes[k], k, k, tiled=True)]
  transfers between devices with their start and end apart: 6 -> 51, of which waited for: 6 -> 31; matrix products, arithmetic and copies ran while one was open for 2% -> 17% of each run, Pallas kernels for 0% -> 0%
where the time goes in v1:
time: 508 us; the launch traced here: 498 us
  waiting for transfers between devices  254 us (50%)
  starting transfers between devices  111 us (22%)
  matrix products  95.3 us (19%)
  other arithmetic  21.6 us (4%)
  local copies, waits for them, and re-layouts  13.2 us (3%)
    all_to_all x10, waiting for transfers between devices, exchange(): lax.all_to_all(parts, PLANE, split_axis=0, concat_axis=0, tiled=True)  174 us
    ppermute x40, waiting for transfers between devices, step_ring(): lax.ppermute(block, RING, [(i, (i + step) % count) for i in range(count)])  75.7 us
    ppermute x40, starting transfers between devices, step_ring(): lax.ppermute(block, RING, [(i, (i + step) % count) for i in range(count)])  55.8 us
    all_to_all x10, starting transfers between devices, exchange(): lax.all_to_all(parts, PLANE, split_axis=0, concat_axis=0, tiled=True)  42.9 us
    dot_general x6, matrix products, transposed(): lax.dot_general(left, right, (((1,), (1,)), ((), ())), preferred_element_...  33.9 us
    dot_general x2, matrix products, expert_forward(): jnp.dot(hidden, w_down, preferred_element_type=jnp.float32)  15.8 us
    dot_general x6, matrix products, pick(): jnp.dot(picking, tokens, preferred_element_type=jnp.float32)  14.1 us
    ppermute x1, starting transfers between devices, body(): arrived = lax.ppermute(produced, 'segment', [(0, 1), (1, 0)])  12.2 us
  transfers between devices with their start and end apart: 51, of which 31 were waited for; matrix products, arithmetic and copies ran while one was open for 17% of the time, Pallas kernels for 0%

profile of v1, /device:TPU:96, one launch (start us, length us, event | category | flops | bytes accessed | tf_op | source)
XLA Modules:
  0.0 497.8 jit_solution(3712819890576408327)
XLA Ops:
  2.6 3.2 collective-permute-start.3
  7.6 3.3 collective-permute-start
  12.4 3.7 collective-permute-start.5
  18.4 3.7 collective-permute-start.2
  24.0 3.8 collective-permute-start.12
  31.2 3.9 collective-permute-start.7
  36.1 3.3 collective-permute-start.14
  42.1 3.8 collective-permute-start.9
  48.5 3.7 collective-permute-done.10
  57.7 7.0 %all-to-all-start.3 = ((bf16[16,24,2048]{2,1,0:T(8,128)(2,1)}), bf16[16,24,2048]{2,1,0:T(8,128)(2,1)S(1)}, u32[]{:S(2)}, u32[]{:S(2)}) async-start(bf16[16,24,2048]{2,1,0:T(8,128)(2,1)} %bitcast.22), calls=%async_computation.3 | async-start | bytes 3145728 | tf_op jit(solution)/shard_map/all_to_all | solution.py:51
  66.5 22.0 %all-to-all-done.3 = bf16[16,24,2048]{2,1,0:T(8,128)(2,1)S(1)} async-done(((bf16[16,24,2048]{2,1,0:T(8,128)(2,1)}), bf16[16,24,2048]{2,1,0:T(8,128)(2,1)S(1)}, u32[]{:S(2)}, u32[]{:S(2)}) %all-to-all-start.3) | async-done | bytes 1572896 | tf_op jit(solution)/shard_map/all_to_all | solution.py:51
  88.4 3.7 all-to-all-start.4
  92.2 3.0 convolution_convert_fusion.4
  95.1 20.7 %all-to-all-done.4 = bf16[16,24,2048]{2,1,0:T(8,128)(2,1)S(1)} async-done(((bf16[16,24,2048]{2,1,0:T(8,128)(2,1)}), bf16[16,24,2048]{2,1,0:T(8,128)(2,1)S(1)}, u32[]{:S(2)}, u32[]{:S(2)}) %all-to-all-start.4) | async-done | bytes 1572896 | tf_op jit(solution)/shard_map/all_to_all | solution.py:51
  117.0 3.7 all-to-all-start.1
  120.7 12.9 %conditional.9 = (bf16[384,2048]{1,0:T(8,128)(2,1)}) conditional(s32[]{:T(128)} %convert_element_type.332, (bf16[384,2048]{1,0:T(8,128)(2,1)S(1)}, bf16[768,2048]{1,0:T(8,128)(2,1)}, bf16[384,2048]{1,0:T(8,128)(2,1)}, bf16[2048,768]{1,0:T(8,128)(2,1)}, bf16[2048,768]{1,0:T(8,128)(2,1)}) %tuple.123, (bf16[384,2048]{1,0:T(8,128)(2,1)}, ...), branch_computations={%region_10.11_spmd, %region_11.12_spmd} | conditional | flops 6046089216 | bytes 47972388
  120.9 4.8 fusion.178
  125.7 7.9 %fusion.19 = bf16[384,2048]{1,0:T(8,128)(2,1)} fusion(bf16[768,2048]{1,0:T(8,128)(2,1)} %get-tuple-element.114, bf16[384,2048]{1,0:T(8,128)(2,1)} %get-tuple-element.111, bf16[2048,768]{1,0:T(8,128)(2,1)} %get-tuple-element.113, f32[384,768]{1,0:T(8,128)} %fusion.178), kind=kOutput, calls=%fused_computation.29 | convolution fusion | flops 2417688576 | bytes 10616832 | tf_op jit(solution)/shard_map/cond/branch_1_fun/dot_general | solution.py:104
  133.6 10.7 %all-to-all-done.1 = bf16[16,24,2048]{2,1,0:T(8,128)(2,1)S(1)} async-done(((bf16[16,24,2048]{2,1,0:T(8,128)(2,1)}), bf16[16,24,2048]{2,1,0:T(8,128)(2,1)S(1)}, u32[]{:S(2)}, u32[]{:S(2)}) %all-to-all-start.1) | async-done | bytes 1572896 | tf_op jit(solution)/shard_map/all_to_all | solution.py:51
  145.5 4.4 all-to-all-start.5
  150.0 3.0 convolution_convert_fusion.5
  153.0 20.7 %all-to-all-done.5 = bf16[16,24,2048]{2,1,0:T(8,128)(2,1)} async-done(((bf16[16,24,2048]{2,1,0:T(8,128)(2,1)}), bf16[16,24,2048]{2,1,0:T(8,128)(2,1)}, u32[]{:S(2)}, u32[]{:S(2)}) %all-to-all-start.5) | async-done | bytes 1572896 | tf_op jit(solution)/shard_map/all_to_all | solution.py:51
  173.7 3.8 all-to-all-start
  177.6 3.6 fusion.171
  183.9 17.3 %all-to-all-done = bf16[16,24,2048]{2,1,0:T(8,128)(2,1)S(1)} async-done(((bf16[16,24,2048]{2,1,0:T(8,128)(2,1)}), bf16[16,24,2048]{2,1,0:T(8,128)(2,1)S(1)}, u32[]{:S(2)}, u32[]{:S(2)}) %all-to-all-start) | async-done | bytes 1572896 | tf_op jit(solution)/shard_map/all_to_all | solution.py:51
  201.2 13.1 %conditional.8 = (bf16[384,2048]{1,0:T(8,128)(2,1)}) conditional(s32[]{:T(128)} %convert_element_type.332, (bf16[384,2048]{1,0:T(8,128)(2,1)S(1)}, bf16[768,2048]{1,0:T(8,128)(2,1)}, bf16[384,2048]{1,0:T(8,128)(2,1)}, bf16[2048,768]{1,0:T(8,128)(2,1)}, bf16[2048,768]{1,0:T(8,128)(2,1)}) %tuple.125, (bf16[384,2048]{1,0:T(8,128)(2,1)}, ...), branch_computations={%region_5.6_spmd, %region_6.7_spmd} | conditional | flops 6046089216 | bytes 47972388
  201.6 4.8 fusion.175
  206.3 7.9 %fusion.8 = bf16[384,2048]{1,0:T(8,128)(2,1)} fusion(bf16[768,2048]{1,0:T(8,128)(2,1)} %get-tuple-element.105, bf16[384,2048]{1,0:T(8,128)(2,1)} %get-tuple-element.102, bf16[2048,768]{1,0:T(8,128)(2,1)} %get-tuple-element.104, f32[384,768]{1,0:T(8,128)} %fusion.175), kind=kOutput, calls=%fused_computation.13 | convolution fusion | flops 2417688576 | bytes 10616832 | tf_op jit(solution)/shard_map/cond/branch_1_fun/dot_general | solution.py:104
  214.2 4.4 all-to-all-start.2
  222.7 5.7 %collective-permute-done.17 = bf16[64,2048]{1,0:T(8,128)(2,1)S(1)} collective-permute-done((bf16[64,2048]{1,0:T(8,128)(2,1)S(1)}, bf16[64,2048]{1,0:T(8,128)(2,1)S(1)}, u32[]{:S(2)}, u32[]{:S(2)}) %collective-permute-start.17) | collective-permute-done | bytes 262176 | tf_op jit(solution)/shard_map/ppermute | solution.py:19
  231.8 10.5 %all-to-all-done.2 = bf16[16,24,2048]{2,1,0:T(8,128)(2,1)} async-done(((bf16[16,24,2048]{2,1,0:T(8,128)(2,1)}), bf16[16,24,2048]{2,1,0:T(8,128)(2,1)}, u32[]{:S(2)}, u32[]{:S(2)}) %all-to-all-start.2) | async-done | bytes 1572896 | tf_op jit(solution)/shard_map/all_to_all | solution.py:51
  245.9 3.2 collective-permute-start.19
  249.2 5.8 %collective-permute-done.22 = bf16[64,2048]{1,0:T(8,128)(2,1)S(1)} collective-permute-done((bf16[64,2048]{1,0:T(8,128)(2,1)S(1)}, bf16[64,2048]{1,0:T(8,128)(2,1)S(1)}, u32[]{:S(2)}, u32[]{:S(2)}) %collective-permute-start.22) | collective-permute-done | bytes 262176 | tf_op jit(solution)/shard_map/ppermute | solution.py:19
  255.8 7.4 %collective-permute-done.23 = bf16[64,2048]{1,0:T(8,128)(2,1)S(1)} collective-permute-done((bf16[64,2048]{1,0:T(8,128)(2,1)S(1)}, bf16[64,2048]{1,0:T(8,128)(2,1)S(1)}, u32[]{:S(2)}, u32[]{:S(2)}) %collective-permute-start.23) | collective-permute-done | bytes 262176 | tf_op jit(solution)/shard_map/ppermute | solution.py:19
  263.9 12.2 %collective-permute-start.24 = (bf16[64,2048]{1,0:T(8,128)(2,1)S(1)}, bf16[64,2048]{1,0:T(8,128)(2,1)S(1)}, u32[]{:S(2)}, u32[]{:S(2)}) collective-permute-start(bf16[64,2048]{1,0:T(8,128)(2,1)S(1)} %fusion.71), channel_id=1, source_target_pairs={{0,128},{128,0},{1,129},{129,1},{2,130},{130,2},{3,131},{131,3},{4... | collective-permute-start | bytes 786440 | tf_op jit(solution)/shard_map/ppermute | solution.py:193
  276.1 4.4 collective-permute-done.24
  283.5 6.0 %collective-permute-done.25 = bf16[64,2048]{1,0:T(8,128)(2,1)S(1)} collective-permute-done((bf16[64,2048]{1,0:T(8,128)(2,1)S(1)}, bf16[64,2048]{1,0:T(8,128)(2,1)S(1)}, u32[]{:S(2)}, u32[]{:S(2)}) %collective-permute-start.25) | collective-permute-done | bytes 262176 | tf_op jit(solution)/shard_map/ppermute | solution.py:19
  291.6 7.1 %collective-permute-done.27 = bf16[64,2048]{1,0:T(8,128)(2,1)S(1)} collective-permute-done((bf16[64,2048]{1,0:T(8,128)(2,1)S(1)}, bf16[64,2048]{1,0:T(8,128)(2,1)S(1)}, u32[]{:S(2)}, u32[]{:S(2)}) %collective-permute-start.27) | collective-permute-done | bytes 262176 | tf_op jit(solution)/shard_map/ppermute | solution.py:19
  300.8 5.0 collective-permute-done.29
  308.0 2.8 collective-permute-done.31
  310.8 3.2 collective-permute-done.32
  315.8 4.4 all-to-all-start.8
  320.2 23.7 %all-to-all-done.8 = bf16[16,24,2048]{2,1,0:T(8,128)(2,1)} async-done(((bf16[16,24,2048]{2,1,0:T(8,128)(2,1)}), bf16[16,24,2048]{2,1,0:T(8,128)(2,1)}, u32[]{:S(2)}, u32[]{:S(2)}) %all-to-all-start.8) | async-done | bytes 1572896 | tf_op jit(solution)/shard_map/all_to_all | solution.py:51
  346.3 22.6 %conditional.11 = (bf16[384,2048]{1,0:T(8,128)(2,1)S(1)}) conditional(s32[]{:T(128)} %convert_element_type.371, (bf16[384,2048]{1,0:T(8,128)(2,1)}, bf16[768,2048]{1,0:T(8,128)(2,1)S(1)}, bf16[384,2048]{1,0:T(8,128)(2,1)S(1)}, bf16[2048,768]{1,0:T(8,128)(2,1)}, bf16[2048,768]{1,0:T(8,128)(2,1)}) %tuple.127, (bf16[384,2048]{1,0:T(8,128)(2,1)S(1)}, ...), branch_computations={%region_19.20_spmd, %region_20.21_spmd} | conditional | flops 6046089216 | bytes 47972416
  346.7 5.0 %fusion.183 = f32[384,768]{1,0:T(8,128)} fusion(bf16[384,2048]{1,0:T(8,128)(2,1)S(1)} %get-tuple-element.126, bf16[2048,768]{1,0:T(8,128)(2,1)} %get-tuple-element.128), kind=kOutput, calls=%fused_computation.314 | convolution fusion | flops 1207959552 | bytes 5898240 | tf_op jit(solution)/shard_map/cond/branch_0_fun/dot_general | solution.py:108
  351.6 4.0 fusion.182
  355.6 8.2 %fusion.35 = f32[384,2048]{1,0:T(8,128)} fusion(bf16[2048,768]{1,0:T(8,128)(2,1)} %get-tuple-element.128, f32[384,768]{1,0:T(8,128)} %fusion.182, bf16[384,2048]{1,0:T(8,128)(2,1)S(1)} %copy-done.10, bf16[2048,768]{1,0:T(8,128)(2,1)} %get-tuple-element.127, f32[384,768]{1,0:T(8,128)} %fusion.183), kind=kOutput, calls=%fused_computation.54 | convolution fusion | flops 2418868224 | bytes 13369344 | tf_op jit(solution)/shard_map/cond/branch_0_fun/dot_general | solution.py:95
  363.9 5.0 convolution_add_fusion.3
  370.0 3.8 all-to-all-start.9
  373.9 2.9 convolution_convert_fusion.1
  376.8 20.7 %all-to-all-done.9 = bf16[16,24,2048]{2,1,0:T(8,128)(2,1)S(1)} async-done(((bf16[16,24,2048]{2,1,0:T(8,128)(2,1)}), bf16[16,24,2048]{2,1,0:T(8,128)(2,1)S(1)}, u32[]{:S(2)}, u32[]{:S(2)}) %all-to-all-start.9) | async-done | bytes 1572896 | tf_op jit(solution)/shard_map/all_to_all | solution.py:51
  398.7 3.7 all-to-all-start.6
  402.4 3.6 fusion.172
  408.9 17.1 %all-to-all-done.6 = bf16[16,24,2048]{2,1,0:T(8,128)(2,1)S(1)} async-done(((bf16[16,24,2048]{2,1,0:T(8,128)(2,1)}), bf16[16,24,2048]{2,1,0:T(8,128)(2,1)S(1)}, u32[]{:S(2)}, u32[]{:S(2)}) %all-to-all-start.6) | async-done | bytes 1572896 | tf_op jit(solution)/shard_map/all_to_all | solution.py:51
  428.0 21.7 %conditional.10 = (bf16[384,2048]{1,0:T(8,128)(2,1)}) conditional(s32[]{:T(128)} %convert_element_type.371, (bf16[384,2048]{1,0:T(8,128)(2,1)S(1)}, bf16[768,2048]{1,0:T(8,128)(2,1)S(1)}, bf16[384,2048]{1,0:T(8,128)(2,1)S(1)}, bf16[2048,768]{1,0:T(8,128)(2,1)}, bf16[2048,768]{1,0:T(8,128)(2,1)}) %tuple.129, (bf16[384,2048]{1,0:T(8,128)(2,1)S(1)}, ...), branch_computations={%region_16.17_spmd, %region_17.18_spmd} | conditional | flops 6046089216 | bytes 52691036
  428.0 5.0 %fusion.180 = f32[384,768]{1,0:T(8,128)} fusion(bf16[384,2048]{1,0:T(8,128)(2,1)S(1)} %get-tuple-element.117, bf16[2048,768]{1,0:T(8,128)(2,1)} %get-tuple-element.119), kind=kOutput, calls=%fused_computation.311 | convolution fusion | flops 1207959552 | bytes 5898240 | tf_op jit(solution)/shard_map/cond/branch_0_fun/dot_general | solution.py:108
  435.4 8.3 %fusion.24 = f32[384,2048]{1,0:T(8,128)} fusion(bf16[2048,768]{1,0:T(8,128)(2,1)} %get-tuple-element.119, f32[384,768]{1,0:T(8,128)} %fusion.179, bf16[384,2048]{1,0:T(8,128)(2,1)S(1)} %copy-done.7, bf16[2048,768]{1,0:T(8,128)(2,1)} %get-tuple-element.118, f32[384,768]{1,0:T(8,128)} %fusion.180), kind=kOutput, calls=%fused_computation.38 | convolution fusion | flops 2418868224 | bytes 13369344 | tf_op jit(solution)/shard_map/cond/branch_0_fun/dot_general | solution.py:95
  443.8 5.8 %convolution_add_fusion.2 = bf16[384,2048]{1,0:T(8,128)(2,1)} fusion(f32[384,2048]{1,0:T(8,128)} %fusion.24, bf16[2048,768]{1,0:T(8,128)(2,1)} %get-tuple-element.118, f32[384,768]{1,0:T(8,128)} %fusion.179, f32[384,768]{1,0:T(8,128)S(1)} %copy-done.65), kind=kOutput, calls=%fused_computation.32 | convolution fusion | flops 1211301888 | bytes 10223616 | tf_op jit(solution)/shard_map/cond/branch_0_fun/dot_general | solution.py:95
  449.6 3.8 all-to-all-start.7
  456.9 6.4 %collective-permute-done.34 = bf16[64,2048]{1,0:T(8,128)(2,1)S(1)} collective-permute-done((bf16[64,2048]{1,0:T(8,128)(2,1)S(1)}, bf16[64,2048]{1,0:T(8,128)(2,1)S(1)}, u32[]{:S(2)}, u32[]{:S(2)}) %collective-permute-start.34) | collective-permute-done | bytes 262176 | tf_op jit(solution)/shard_map/ppermute | solution.py:19
  466.1 11.0 %all-to-all-done.7 = bf16[16,24,2048]{2,1,0:T(8,128)(2,1)S(1)} async-done(((bf16[16,24,2048]{2,1,0:T(8,128)(2,1)}), bf16[16,24,2048]{2,1,0:T(8,128)(2,1)S(1)}, u32[]{:S(2)}, u32[]{:S(2)}) %all-to-all-start.7) | async-done | bytes 1572896 | tf_op jit(solution)/shard_map/all_to_all | solution.py:51
  478.9 3.2 collective-permute-start.36
  482.1 5.8 %collective-permute-done.39 = bf16[64,2048]{1,0:T(8,128)(2,1)S(1)} collective-permute-done((bf16[64,2048]{1,0:T(8,128)(2,1)S(1)}, bf16[64,2048]{1,0:T(8,128)(2,1)S(1)}, u32[]{:S(2)}, u32[]{:S(2)}) %collective-permute-start.39) | collective-permute-done | bytes 262176 | tf_op jit(solution)/shard_map/ppermute | solution.py:19
  488.1 8.1 %collective-permute-done.40 = bf16[64,2048]{1,0:T(8,128)(2,1)S(1)} collective-permute-done((bf16[64,2048]{1,0:T(8,128)(2,1)S(1)}, bf16[64,2048]{1,0:T(8,128)(2,1)S(1)}, u32[]{:S(2)}, u32[]{:S(2)}) %collective-permute-start.40) | collective-permute-done | bytes 262176 | tf_op jit(solution)/shard_map/ppermute | solution.py:19
  (268 shorter events, 76.9 us)
Async XLA Ops:
  1.3 29.4 %copy-start.1 = (bf16[64,2048]{1,0:T(8,128)(2,1)}, bf16[64,2048]{1,0:T(8,128)(2,1)S(1)}, u32[]{:S(2)}) copy-start(bf16[64,2048]{1,0:T(8,128)(2,1)S(1)} %get-tuple-element.150) | copy-start | bytes 786436
  2.6 20.8 %copy-start.22 = (bf16[64,2048]{1,0:T(8,128)(2,1)}, bf16[64,2048]{1,0:T(8,128)(2,1)S(1)}, u32[]{:S(2)}) copy-start(bf16[64,2048]{1,0:T(8,128)(2,1)S(1)} %fusion.97) | copy-start | bytes 786436
  2.6 9.8 %collective-permute-start.3 = (bf16[64,2048]{1,0:T(8,128)(2,1)S(1)}, bf16[64,2048]{1,0:T(8,128)(2,1)S(1)}, u32[]{:S(2)}, u32[]{:S(2)}) collective-permute-start(bf16[64,2048]{1,0:T(8,128)(2,1)S(1)} %fusion.97), channel_id=1, source_target_pairs={{0,2},{2,4},{4,6},{6,8},{8,10},{10,12},{12,14},{14,0},{1,3},{3,5},... | collective-permute-start | bytes 786440 | tf_op jit(solution)/shard_map/ppermute | solution.py:19
  5.8 10.3 %collective-permute-start.4 = (bf16[64,2048]{1,0:T(8,128)(2,1)S(1)}, bf16[64,2048]{1,0:T(8,128)(2,1)S(1)}, u32[]{:S(2)}, u32[]{:S(2)}) collective-permute-start(bf16[64,2048]{1,0:T(8,128)(2,1)S(1)} %fusion.97), channel_id=1, source_target_pairs={{0,14},{2,0},{4,2},{6,4},{8,6},{10,8},{12,10},{14,12},{1,15},{3,1}... | collective-permute-start | bytes 786440 | tf_op jit(solution)/shard_map/ppermute | solution.py:19
  6.0 22.8 %copy-start.18 = (s32[1,1,64,8]{3,2,1,0:T(8,128)}, s32[1,1,64,8]{3,2,1,0:T(8,128)S(1)}, u32[]{:S(2)}) copy-start(s32[1,1,64,8]{3,2,1,0:T(8,128)S(1)} %copy.36) | copy-start | bytes 6148
  7.6 23.3 %copy-start.25 = (bf16[64,128]{1,0:T(8,128)(2,1)}, bf16[64,128]{1,0:T(8,128)(2,1)S(1)}, u32[]{:S(2)}) copy-start(bf16[64,128]{1,0:T(8,128)(2,1)S(1)} %fusion.143) | copy-start | bytes 49156
  7.6 10.8 %collective-permute-start = (bf16[64,2176]{1,0:T(8,128)(2,1)S(1)}, bf16[64,2176]{1,0:T(8,128)(2,1)S(1)}, u32[]{:S(2)}, u32[]{:S(2)}) collective-permute-start(bf16[64,2176]{1,0:T(8,128)(2,1)S(1)} %pad_maximum_fusion.8), channel_id=1, source_target_pairs={{0,2},{2,4},{4,6},{6,8},{8,10},{10,12},{12,14},{14,0},{1,3},{3,5},... | collective-permute-start | bytes 835592 | tf_op jit(solution)/shard_map/ppermute | solution.py:19
  10.9 12.4 %collective-permute-start.1 = (bf16[64,2176]{1,0:T(8,128)(2,1)S(1)}, bf16[64,2176]{1,0:T(8,128)(2,1)S(1)}, u32[]{:S(2)}, u32[]{:S(2)}) collective-permute-start(bf16[64,2176]{1,0:T(8,128)(2,1)S(1)} %pad_maximum_fusion.8), channel_id=1, source_target_pairs={{0,14},{2,0},{4,2},{6,4},{8,6},{10,8},{12,10},{14,12},{1,15},{3,1}... | collective-permute-start | bytes 835592 | tf_op jit(solution)/shard_map/ppermute | solution.py:19
  12.4 11.6 %collective-permute-start.5 = (bf16[64,2048]{1,0:T(8,128)(2,1)S(1)}, bf16[64,2048]{1,0:T(8,128)(2,1)}, u32[]{:S(2)}, u32[]{:S(2)}) collective-permute-start(bf16[64,2048]{1,0:T(8,128)(2,1)S(1)} %collective-permute-done.3), channel_id=1, source_target_pairs={{0,2},{2,4},{4,6},{6,8},{8,10},{10,12},{12,14},{14,0},{1,3},{3,5},... | collective-permute-start | bytes 786440 | tf_op jit(solution)/shard_map/ppermute | solution.py:19
  16.1 11.7 %collective-permute-start.11 = (bf16[64,2048]{1,0:T(8,128)(2,1)S(1)}, bf16[64,2048]{1,0:T(8,128)(2,1)}, u32[]{:S(2)}, u32[]{:S(2)}) collective-permute-start(bf16[64,2048]{1,0:T(8,128)(2,1)S(1)} %collective-permute-done.4), channel_id=1, source_target_pairs={{0,14},{2,0},{4,2},{6,4},{8,6},{10,8},{12,10},{14,12},{1,15},{3,1}... | collective-permute-start | bytes 786440 | tf_op jit(solution)/shard_map/ppermute | solution.py:19
  18.4 11.6 %collective-permute-start.2 = (bf16[64,2176]{1,0:T(8,128)(2,1)S(1)}, bf16[64,2176]{1,0:T(8,128)(2,1)}, u32[]{:S(2)}, u32[]{:S(2)}) collective-permute-start(bf16[64,2176]{1,0:T(8,128)(2,1)S(1)} %collective-permute-done), channel_id=1, source_target_pairs={{0,2},{2,4},{4,6},{6,8},{8,10},{10,12},{12,14},{14,0},{1,3},{3,5},... | collective-permute-start | bytes 835592 | tf_op jit(solution)/shard_map/ppermute | solution.py:19
  23.4 11.7 %collective-permute-start.6 = (bf16[64,2176]{1,0:T(8,128)(2,1)S(1)}, bf16[64,2176]{1,0:T(8,128)(2,1)}, u32[]{:S(2)}, u32[]{:S(2)}) collective-permute-start(bf16[64,2176]{1,0:T(8,128)(2,1)S(1)} %collective-permute-done.1), channel_id=1, source_target_pairs={{0,14},{2,0},{4,2},{6,4},{8,6},{10,8},{12,10},{14,12},{1,15},{3,1}... | collective-permute-start | bytes 835592 | tf_op jit(solution)/shard_map/ppermute | solution.py:19
  24.0 12.0 %collective-permute-start.12 = (bf16[64,2048]{1,0:T(8,128)(2,1)}, bf16[64,2048]{1,0:T(8,128)(2,1)S(1)}, u32[]{:S(2)}, u32[]{:S(2)}) collective-permute-start(bf16[64,2048]{1,0:T(8,128)(2,1)} %collective-permute-done.5), channel_id=1, source_target_pairs={{0,2},{2,4},{4,6},{6,8},{8,10},{10,12},{12,14},{14,0},{1,3},{3,5},... | collective-permute-start | bytes 786440 | tf_op jit(solution)/shard_map/ppermute | solution.py:19
  27.8 11.6 %collective-permute-start.13 = (bf16[64,2048]{1,0:T(8,128)(2,1)}, bf16[64,2048]{1,0:T(8,128)(2,1)S(1)}, u32[]{:S(2)}, u32[]{:S(2)}) collective-permute-start(bf16[64,2048]{1,0:T(8,128)(2,1)} %collective-permute-done.11), channel_id=1, source_target_pairs={{0,14},{2,0},{4,2},{6,4},{8,6},{10,8},{12,10},{14,12},{1,15},{3,1}... | collective-permute-start | bytes 786440 | tf_op jit(solution)/shard_map/ppermute | solution.py:19
  31.2 10.9 %collective-permute-start.7 = (bf16[64,2176]{1,0:T(8,128)(2,1)}, bf16[64,2176]{1,0:T(8,128)(2,1)S(1)}, u32[]{:S(2)}, u32[]{:S(2)}) collective-permute-start(bf16[64,2176]{1,0:T(8,128)(2,1)} %collective-permute-done.2), channel_id=1, source_target_pairs={{0,2},{2,4},{4,6},{6,8},{8,10},{10,12},{12,14},{14,0},{1,3},{3,5},... | collective-permute-start | bytes 835592 | tf_op jit(solution)/shard_map/ppermute | solution.py:19
  35.0 10.9 %collective-permute-start.8 = (bf16[64,2176]{1,0:T(8,128)(2,1)}, bf16[64,2176]{1,0:T(8,128)(2,1)S(1)}, u32[]{:S(2)}, u32[]{:S(2)}) collective-permute-start(bf16[64,2176]{1,0:T(8,128)(2,1)} %collective-permute-done.6), channel_id=1, source_target_pairs={{0,14},{2,0},{4,2},{6,4},{8,6},{10,8},{12,10},{14,12},{1,15},{3,1}... | collective-permute-start | bytes 835592 | tf_op jit(solution)/shard_map/ppermute | solution.py:19
  36.1 10.1 %collective-permute-start.14 = (bf16[32,2048]{1,0:T(8,128)(2,1)S(1)}, bf16[32,2048]{1,0:T(8,128)(2,1)S(1)}, u32[]{:S(2)}, u32[]{:S(2)}) collective-permute-start(bf16[32,2048]{1,0:T(8,128)(2,1)S(1)} %slice.239), channel_id=1, source_target_pairs={{0,2},{2,4},{4,6},{6,8},{8,10},{10,12},{12,14},{14,0},{1,3},{3,5},... | collective-permute-start | bytes 393224 | tf_op jit(solution)/shard_map/ppermute | solution.py:19
  39.4 7.6 %collective-permute-start.15 = (bf16[32,2048]{1,0:T(8,128)(2,1)S(1)}, bf16[32,2048]{1,0:T(8,128)(2,1)S(1)}, u32[]{:S(2)}, u32[]{:S(2)}) collective-permute-start(bf16[32,2048]{1,0:T(8,128)(2,1)S(1)} %slice.240), channel_id=1, source_target_pairs={{0,14},{2,0},{4,2},{6,4},{8,6},{10,8},{12,10},{14,12},{1,15},{3,1}... | collective-permute-start | bytes 393224 | tf_op jit(solution)/shard_map/ppermute | solution.py:19
  42.1 6.4 %collective-permute-start.9 = (bf16[32,2176]{1,0:T(8,128)(2,1)S(1)}, bf16[32,2176]{1,0:T(8,128)(2,1)S(1)}, u32[]{:S(2)}, u32[]{:S(2)}) collective-permute-start(bf16[32,2176]{1,0:T(8,128)(2,1)S(1)} %slice.233), channel_id=1, source_target_pairs={{0,2},{2,4},{4,6},{6,8},{8,10},{10,12},{12,14},{14,0},{1,3},{3,5},... | collective-permute-start | bytes 417800 | tf_op jit(solution)/shard_map/ppermute | solution.py:19
  45.9 6.3 %collective-permute-start.10 = (bf16[32,2176]{1,0:T(8,128)(2,1)S(1)}, bf16[32,2176]{1,0:T(8,128)(2,1)S(1)}, u32[]{:S(2)}, u32[]{:S(2)}) collective-permute-start(bf16[32,2176]{1,0:T(8,128)(2,1)S(1)} %slice.234), channel_id=1, source_target_pairs={{0,14},{2,0},{4,2},{6,4},{8,6},{10,8},{12,10},{14,12},{1,15},{3,1}... | collective-permute-start | bytes 417800 | tf_op jit(solution)/shard_map/ppermute | solution.py:19
  57.7 30.7 %all-to-all-start.3 = ((bf16[16,24,2048]{2,1,0:T(8,128)(2,1)}), bf16[16,24,2048]{2,1,0:T(8,128)(2,1)S(1)}, u32[]{:S(2)}, u32[]{:S(2)}) async-start(bf16[16,24,2048]{2,1,0:T(8,128)(2,1)} %bitcast.22), calls=%async_computation.3 | async-start | bytes 3145728 | tf_op jit(solution)/shard_map/all_to_all | solution.py:51
  88.4 27.4 %all-to-all-start.4 = ((bf16[16,24,2048]{2,1,0:T(8,128)(2,1)}), bf16[16,24,2048]{2,1,0:T(8,128)(2,1)S(1)}, u32[]{:S(2)}, u32[]{:S(2)}) async-start(bf16[16,24,2048]{2,1,0:T(8,128)(2,1)} %bitcast.24), calls=%async_computation.4 | async-start | bytes 3145728 | tf_op jit(solution)/shard_map/all_to_all | solution.py:51
  117.0 27.4 %all-to-all-start.1 = ((bf16[16,24,2048]{2,1,0:T(8,128)(2,1)}), bf16[16,24,2048]{2,1,0:T(8,128)(2,1)S(1)}, u32[]{:S(2)}, u32[]{:S(2)}) async-start(bf16[16,24,2048]{2,1,0:T(8,128)(2,1)} %bitcast.141), calls=%async_computation.1 | async-start | bytes 3145728 | tf_op jit(solution)/shard_map/all_to_all | solution.py:51
  145.5 28.1 %all-to-all-start.5 = ((bf16[16,24,2048]{2,1,0:T(8,128)(2,1)}), bf16[16,24,2048]{2,1,0:T(8,128)(2,1)}, u32[]{:S(2)}, u32[]{:S(2)}) async-start(bf16[16,24,2048]{2,1,0:T(8,128)(2,1)} %bitcast.146), calls=%async_computation.5 | async-start | bytes 3145728 | tf_op jit(solution)/shard_map/all_to_all | solution.py:51
  173.7 27.5 %all-to-all-start = ((bf16[16,24,2048]{2,1,0:T(8,128)(2,1)}), bf16[16,24,2048]{2,1,0:T(8,128)(2,1)S(1)}, u32[]{:S(2)}, u32[]{:S(2)}) async-start(bf16[16,24,2048]{2,1,0:T(8,128)(2,1)} %bitcast.144), calls=%async_computation | async-start | bytes 3145728 | tf_op jit(solution)/shard_map/all_to_all | solution.py:51
  181.9 36.8 %collective-permute-start.16 = (bf16[32,2048]{1,0:T(8,128)(2,1)}, bf16[32,2048]{1,0:T(8,128)(2,1)}, u32[]{:S(2)}, u32[]{:S(2)}) collective-permute-start(bf16[32,2048]{1,0:T(8,128)(2,1)} %get-tuple-element.163), channel_id=1, source_target_pairs={{0,2},{2,4},{4,6},{6,8},{8,10},{10,12},{12,14},{14,0},{1,3},{3,5},... | collective-permute-start | bytes 393224 | tf_op jit(solution)/shard_map/ppermute | solution.py:19
  181.9 36.8 %collective-permute-start.20 = (bf16[32,2048]{1,0:T(8,128)(2,1)}, bf16[32,2048]{1,0:T(8,128)(2,1)}, u32[]{:S(2)}, u32[]{:S(2)}) collective-permute-start(bf16[32,2048]{1,0:T(8,128)(2,1)} %get-tuple-element.164), channel_id=1, source_target_pairs={{0,14},{2,0},{4,2},{6,4},{8,6},{10,8},{12,10},{14,12},{1,15},{3,1}... | collective-permute-start | bytes 393224 | tf_op jit(solution)/shard_map/ppermute | solution.py:19
  214.2 28.1 %all-to-all-start.2 = ((bf16[16,24,2048]{2,1,0:T(8,128)(2,1)}), bf16[16,24,2048]{2,1,0:T(8,128)(2,1)}, u32[]{:S(2)}, u32[]{:S(2)}) async-start(bf16[16,24,2048]{2,1,0:T(8,128)(2,1)} %bitcast.147), calls=%async_computation.2 | async-start | bytes 3145728 | tf_op jit(solution)/shard_map/all_to_all | solution.py:51
  219.9 8.5 %collective-permute-start.17 = (bf16[64,2048]{1,0:T(8,128)(2,1)S(1)}, bf16[64,2048]{1,0:T(8,128)(2,1)S(1)}, u32[]{:S(2)}, u32[]{:S(2)}) collective-permute-start(bf16[64,2048]{1,0:T(8,128)(2,1)S(1)} %pad_maximum_fusion.9), channel_id=1, source_target_pairs={{0,2},{2,4},{4,6},{6,8},{8,10},{10,12},{12,14},{14,0},{1,3},{3,5},... | collective-permute-start | bytes 786440 | tf_op jit(solution)/shard_map/ppermute | solution.py:19
  220.7 24.0 %collective-permute-start.21 = (bf16[64,2048]{1,0:T(8,128)(2,1)}, bf16[64,2048]{1,0:T(8,128)(2,1)}, u32[]{:S(2)}, u32[]{:S(2)}) collective-permute-start(bf16[64,2048]{1,0:T(8,128)(2,1)} %pad_maximum_fusion.10), channel_id=1, source_target_pairs={{0,14},{2,0},{4,2},{6,4},{8,6},{10,8},{12,10},{14,12},{1,15},{3,1}... | collective-permute-start | bytes 786440 | tf_op jit(solution)/shard_map/ppermute | solution.py:19
  230.2 14.4 %collective-permute-start.18 = (bf16[64,2048]{1,0:T(8,128)(2,1)}, bf16[64,2048]{1,0:T(8,128)(2,1)}, u32[]{:S(2)}, u32[]{:S(2)}) collective-permute-start(bf16[64,2048]{1,0:T(8,128)(2,1)} %fusion.91), channel_id=1, source_target_pairs={{0,2},{2,4},{4,6},{6,8},{8,10},{10,12},{12,14},{14,0},{1,3},{3,5},... | collective-permute-start | bytes 786440 | tf_op jit(solution)/shard_map/ppermute | solution.py:19
  244.6 18.6 %copy-start.2 = (bf16[64,2048]{1,0:T(8,128)(2,1)S(1)}, bf16[64,2048]{1,0:T(8,128)(2,1)}, u32[]{:S(2)}) copy-start(bf16[64,2048]{1,0:T(8,128)(2,1)} %copy-done.1) | copy-start | bytes 786436
  245.8 17.6 %copy-start.5 = (bf16[1,64,2048]{2,1,0:T(8,128)(2,1)S(1)}, bf16[1,64,2048]{2,1,0:T(8,128)(2,1)}, u32[]{:S(2)}) copy-start(bf16[1,64,2048]{2,1,0:T(8,128)(2,1)} %param.16) | copy-start | bytes 786436
  245.8 17.6 %copy-start.43 = (f32[64]{0:T(128)S(1)}, f32[64]{0:T(128)}, u32[]{:S(2)}) copy-start(f32[64]{0:T(128)} %copy-done.42) | copy-start | bytes 772
  245.8 17.6 %copy-start.48 = (f32[64]{0:T(128)S(1)}, f32[64]{0:T(128)}, u32[]{:S(2)}) copy-start(f32[64]{0:T(128)} %get-tuple-element.190) | copy-start | bytes 772
  245.9 9.1 %collective-permute-start.22 = (bf16[64,2048]{1,0:T(8,128)(2,1)S(1)}, bf16[64,2048]{1,0:T(8,128)(2,1)S(1)}, u32[]{:S(2)}, u32[]{:S(2)}) collective-permute-start(bf16[64,2048]{1,0:T(8,128)(2,1)S(1)} %get-tuple-element.156), channel_id=1, source_target_pairs={{0,14},{2,0},{4,2},{6,4},{8,6},{10,8},{12,10},{14,12},{1,15},{3,1}... | collective-permute-start | bytes 786440 | tf_op jit(solution)/shard_map/ppermute | solution.py:19
  245.9 9.9 %collective-permute-start.19 = (bf16[64,2048]{1,0:T(8,128)(2,1)S(1)}, bf16[64,2048]{1,0:T(8,128)(2,1)S(1)}, u32[]{:S(2)}, u32[]{:S(2)}) collective-permute-start(bf16[64,2048]{1,0:T(8,128)(2,1)S(1)} %get-tuple-element.155), channel_id=1, source_target_pairs={{0,2},{2,4},{4,6},{6,8},{8,10},{10,12},{12,14},{14,0},{1,3},{3,5},... | collective-permute-start | bytes 786440 | tf_op jit(solution)/shard_map/ppermute | solution.py:19
  255.0 8.2 %collective-permute-start.23 = (bf16[64,2048]{1,0:T(8,128)(2,1)S(1)}, bf16[64,2048]{1,0:T(8,128)(2,1)S(1)}, u32[]{:S(2)}, u32[]{:S(2)}) collective-permute-start(bf16[64,2048]{1,0:T(8,128)(2,1)S(1)} %fusion.90), channel_id=1, source_target_pairs={{0,14},{2,0},{4,2},{6,4},{8,6},{10,8},{12,10},{14,12},{1,15},{3,1}... | collective-permute-start | bytes 786440 | tf_op jit(solution)/shard_map/ppermute | solution.py:19
  263.9 16.6 %collective-permute-start.24 = (bf16[64,2048]{1,0:T(8,128)(2,1)S(1)}, bf16[64,2048]{1,0:T(8,128)(2,1)S(1)}, u32[]{:S(2)}, u32[]{:S(2)}) collective-permute-start(bf16[64,2048]{1,0:T(8,128)(2,1)S(1)} %fusion.71), channel_id=1, source_target_pairs={{0,128},{128,0},{1,129},{129,1},{2,130},{130,2},{3,131},{131,3},{4... | collective-permute-start | bytes 786440 | tf_op jit(solution)/shard_map/ppermute | solution.py:193
  280.5 27.5 %copy-start.3 = (bf16[64,2048]{1,0:T(8,128)(2,1)}, bf16[64,2048]{1,0:T(8,128)(2,1)S(1)}, u32[]{:S(2)}) copy-start(bf16[64,2048]{1,0:T(8,128)(2,1)S(1)} %collective-permute-done.24) | copy-start | bytes 786436
  281.2 29.6 %copy-start.44 = (f32[64]{0:T(128)}, f32[64]{0:T(128)S(1)}, u32[]{:S(2)}) copy-start(f32[64]{0:T(128)S(1)} %get-tuple-element.189) | copy-start | bytes 772
  281.4 29.4 %copy-start.24 = (bf16[64,2048]{1,0:T(8,128)(2,1)}, bf16[64,2048]{1,0:T(8,128)(2,1)S(1)}, u32[]{:S(2)}) copy-start(bf16[64,2048]{1,0:T(8,128)(2,1)S(1)} %fusion.96) | copy-start | bytes 786436
  281.4 8.1 %collective-permute-start.25 = (bf16[64,2048]{1,0:T(8,128)(2,1)S(1)}, bf16[64,2048]{1,0:T(8,128)(2,1)S(1)}, u32[]{:S(2)}, u32[]{:S(2)}) collective-permute-start(bf16[64,2048]{1,0:T(8,128)(2,1)S(1)} %fusion.96), channel_id=1, source_target_pairs={{0,2},{2,4},{4,6},{6,8},{8,10},{10,12},{12,14},{14,0},{1,3},{3,5},... | collective-permute-start | bytes 786440 | tf_op jit(solution)/shard_map/ppermute | solution.py:19
  281.5 8.0 %collective-permute-start.26 = (bf16[64,2048]{1,0:T(8,128)(2,1)S(1)}, bf16[64,2048]{1,0:T(8,128)(2,1)S(1)}, u32[]{:S(2)}, u32[]{:S(2)}) collective-permute-start(bf16[64,2048]{1,0:T(8,128)(2,1)S(1)} %fusion.96), channel_id=1, source_target_pairs={{0,14},{2,0},{4,2},{6,4},{8,6},{10,8},{12,10},{14,12},{1,15},{3,1}... | collective-permute-start | bytes 786440 | tf_op jit(solution)/shard_map/ppermute | solution.py:19
  289.5 9.2 %collective-permute-start.27 = (bf16[64,2048]{1,0:T(8,128)(2,1)S(1)}, bf16[64,2048]{1,0:T(8,128)(2,1)S(1)}, u32[]{:S(2)}, u32[]{:S(2)}) collective-permute-start(bf16[64,2048]{1,0:T(8,128)(2,1)S(1)} %collective-permute-done.25), channel_id=1, source_target_pairs={{0,2},{2,4},{4,6},{6,8},{8,10},{10,12},{12,14},{14,0},{1,3},{3,5},... | collective-permute-start | bytes 786440 | tf_op jit(solution)/shard_map/ppermute | solution.py:19
  289.6 9.2 %collective-permute-start.28 = (bf16[64,2048]{1,0:T(8,128)(2,1)S(1)}, bf16[64,2048]{1,0:T(8,128)(2,1)S(1)}, u32[]{:S(2)}, u32[]{:S(2)}) collective-permute-start(bf16[64,2048]{1,0:T(8,128)(2,1)S(1)} %collective-permute-done.26), channel_id=1, source_target_pairs={{0,14},{2,0},{4,2},{6,4},{8,6},{10,8},{12,10},{14,12},{1,15},{3,1}... | collective-permute-start | bytes 786440 | tf_op jit(solution)/shard_map/ppermute | solution.py:19
  298.7 7.0 %collective-permute-start.29 = (bf16[64,2048]{1,0:T(8,128)(2,1)S(1)}, bf16[64,2048]{1,0:T(8,128)(2,1)S(1)}, u32[]{:S(2)}, u32[]{:S(2)}) collective-permute-start(bf16[64,2048]{1,0:T(8,128)(2,1)S(1)} %collective-permute-done.27), channel_id=1, source_target_pairs={{0,2},{2,4},{4,6},{6,8},{8,10},{10,12},{12,14},{14,0},{1,3},{3,5},... | collective-permute-start | bytes 786440 | tf_op jit(solution)/shard_map/ppermute | solution.py:19
  298.8 9.0 %collective-permute-start.30 = (bf16[64,2048]{1,0:T(8,128)(2,1)S(1)}, bf16[64,2048]{1,0:T(8,128)(2,1)S(1)}, u32[]{:S(2)}, u32[]{:S(2)}) collective-permute-start(bf16[64,2048]{1,0:T(8,128)(2,1)S(1)} %collective-permute-done.28), channel_id=1, source_target_pairs={{0,14},{2,0},{4,2},{6,4},{8,6},{10,8},{12,10},{14,12},{1,15},{3,1}... | collective-permute-start | bytes 786440 | tf_op jit(solution)/shard_map/ppermute | solution.py:19
  305.7 5.0 %collective-permute-start.31 = (bf16[32,2048]{1,0:T(8,128)(2,1)S(1)}, bf16[32,2048]{1,0:T(8,128)(2,1)S(1)}, u32[]{:S(2)}, u32[]{:S(2)}) collective-permute-start(bf16[32,2048]{1,0:T(8,128)(2,1)S(1)} %slice.255), channel_id=1, source_target_pairs={{0,2},{2,4},{4,6},{6,8},{8,10},{10,12},{12,14},{14,0},{1,3},{3,5},... | collective-permute-start | bytes 393224 | tf_op jit(solution)/shard_map/ppermute | solution.py:19
  307.8 6.3 %collective-permute-start.32 = (bf16[32,2048]{1,0:T(8,128)(2,1)S(1)}, bf16[32,2048]{1,0:T(8,128)(2,1)S(1)}, u32[]{:S(2)}, u32[]{:S(2)}) collective-permute-start(bf16[32,2048]{1,0:T(8,128)(2,1)S(1)} %slice.256), channel_id=1, source_target_pairs={{0,14},{2,0},{4,2},{6,4},{8,6},{10,8},{12,10},{14,12},{1,15},{3,1}... | collective-permute-start | bytes 393224 | tf_op jit(solution)/shard_map/ppermute | solution.py:19
  315.8 28.1 %all-to-all-start.8 = ((bf16[16,24,2048]{2,1,0:T(8,128)(2,1)}), bf16[16,24,2048]{2,1,0:T(8,128)(2,1)}, u32[]{:S(2)}, u32[]{:S(2)}) async-start(bf16[16,24,2048]{2,1,0:T(8,128)(2,1)} %bitcast.138), calls=%async_computation.8 | async-start | bytes 3145728 | tf_op jit(solution)/shard_map/all_to_all | solution.py:51
  370.0 27.5 %all-to-all-start.9 = ((bf16[16,24,2048]{2,1,0:T(8,128)(2,1)}), bf16[16,24,2048]{2,1,0:T(8,128)(2,1)S(1)}, u32[]{:S(2)}, u32[]{:S(2)}) async-start(bf16[16,24,2048]{2,1,0:T(8,128)(2,1)} %bitcast.148), calls=%async_computation.9 | async-start | bytes 3145728 | tf_op jit(solution)/shard_map/all_to_all | solution.py:51
  398.7 27.4 %all-to-all-start.6 = ((bf16[16,24,2048]{2,1,0:T(8,128)(2,1)}), bf16[16,24,2048]{2,1,0:T(8,128)(2,1)S(1)}, u32[]{:S(2)}, u32[]{:S(2)}) async-start(bf16[16,24,2048]{2,1,0:T(8,128)(2,1)} %bitcast.145), calls=%async_computation.6 | async-start | bytes 3145728 | tf_op jit(solution)/shard_map/all_to_all | solution.py:51
  406.8 46.7 %collective-permute-start.33 = (bf16[32,2048]{1,0:T(8,128)(2,1)}, bf16[32,2048]{1,0:T(8,128)(2,1)}, u32[]{:S(2)}, u32[]{:S(2)}) collective-permute-start(bf16[32,2048]{1,0:T(8,128)(2,1)} %get-tuple-element.159), channel_id=1, source_target_pairs={{0,2},{2,4},{4,6},{6,8},{8,10},{10,12},{12,14},{14,0},{1,3},{3,5},... | collective-permute-start | bytes 393224 | tf_op jit(solution)/shard_map/ppermute | solution.py:19
  406.8 46.7 %collective-permute-start.37 = (bf16[32,2048]{1,0:T(8,128)(2,1)}, bf16[32,2048]{1,0:T(8,128)(2,1)}, u32[]{:S(2)}, u32[]{:S(2)}) collective-permute-start(bf16[32,2048]{1,0:T(8,128)(2,1)} %get-tuple-element.160), channel_id=1, source_target_pairs={{0,14},{2,0},{4,2},{6,4},{8,6},{10,8},{12,10},{14,12},{1,15},{3,1}... | collective-permute-start | bytes 393224 | tf_op jit(solution)/shard_map/ppermute | solution.py:19
  449.6 27.5 %all-to-all-start.7 = ((bf16[16,24,2048]{2,1,0:T(8,128)(2,1)}), bf16[16,24,2048]{2,1,0:T(8,128)(2,1)S(1)}, u32[]{:S(2)}, u32[]{:S(2)}) async-start(bf16[16,24,2048]{2,1,0:T(8,128)(2,1)} %bitcast.30), calls=%async_computation.7 | async-start | bytes 3145728 | tf_op jit(solution)/shard_map/all_to_all | solution.py:51
  454.7 8.6 %collective-permute-start.34 = (bf16[64,2048]{1,0:T(8,128)(2,1)S(1)}, bf16[64,2048]{1,0:T(8,128)(2,1)S(1)}, u32[]{:S(2)}, u32[]{:S(2)}) collective-permute-start(bf16[64,2048]{1,0:T(8,128)(2,1)S(1)} %pad_maximum_fusion.11), channel_id=1, source_target_pairs={{0,2},{2,4},{4,6},{6,8},{8,10},{10,12},{12,14},{14,0},{1,3},{3,5},... | collective-permute-start | bytes 786440 | tf_op jit(solution)/shard_map/ppermute | solution.py:19
  454.8 23.9 %collective-permute-start.38 = (bf16[64,2048]{1,0:T(8,128)(2,1)S(1)}, bf16[64,2048]{1,0:T(8,128)(2,1)S(1)}, u32[]{:S(2)}, u32[]{:S(2)}) collective-permute-start(bf16[64,2048]{1,0:T(8,128)(2,1)S(1)} %pad_maximum_fusion.12), channel_id=1, source_target_pairs={{0,14},{2,0},{4,2},{6,4},{8,6},{10,8},{12,10},{14,12},{1,15},{3,1}... | collective-permute-start | bytes 786440 | tf_op jit(solution)/shard_map/ppermute | solution.py:19
  464.3 14.3 %collective-permute-start.35 = (bf16[64,2048]{1,0:T(8,128)(2,1)S(1)}, bf16[64,2048]{1,0:T(8,128)(2,1)S(1)}, u32[]{:S(2)}, u32[]{:S(2)}) collective-permute-start(bf16[64,2048]{1,0:T(8,128)(2,1)S(1)} %fusion.85), channel_id=1, source_target_pairs={{0,2},{2,4},{4,6},{6,8},{8,10},{10,12},{12,14},{14,0},{1,3},{3,5},... | collective-permute-start | bytes 786440 | tf_op jit(solution)/shard_map/ppermute | solution.py:19
  478.8 17.7 %copy-start.45 = (f32[64]{0:T(128)S(1)}, f32[64]{0:T(128)}, u32[]{:S(2)}) copy-start(f32[64]{0:T(128)} %copy-done.44) | copy-start | bytes 772
  478.8 17.6 %copy-start.50 = (f32[64]{0:T(128)S(1)}, f32[64]{0:T(128)}, u32[]{:S(2)}) copy-start(f32[64]{0:T(128)} %get-tuple-element.188) | copy-start | bytes 772
  478.8 9.1 %collective-permute-start.39 = (bf16[64,2048]{1,0:T(8,128)(2,1)S(1)}, bf16[64,2048]{1,0:T(8,128)(2,1)S(1)}, u32[]{:S(2)}, u32[]{:S(2)}) collective-permute-start(bf16[64,2048]{1,0:T(8,128)(2,1)S(1)} %get-tuple-element.152), channel_id=1, source_target_pairs={{0,14},{2,0},{4,2},{6,4},{8,6},{10,8},{12,10},{14,12},{1,15},{3,1}... | collective-permute-start | bytes 786440 | tf_op jit(solution)/shard_map/ppermute | solution.py:19
  478.9 9.2 %collective-permute-start.36 = (bf16[64,2048]{1,0:T(8,128)(2,1)S(1)}, bf16[64,2048]{1,0:T(8,128)(2,1)S(1)}, u32[]{:S(2)}, u32[]{:S(2)}) collective-permute-start(bf16[64,2048]{1,0:T(8,128)(2,1)S(1)} %get-tuple-element.151), channel_id=1, source_target_pairs={{0,2},{2,4},{4,6},{6,8},{8,10},{10,12},{12,14},{14,0},{1,3},{3,5},... | collective-permute-start | bytes 786440 | tf_op jit(solution)/shard_map/ppermute | solution.py:19
  487.9 8.2 %collective-permute-start.40 = (bf16[64,2048]{1,0:T(8,128)(2,1)S(1)}, bf16[64,2048]{1,0:T(8,128)(2,1)S(1)}, u32[]{:S(2)}, u32[]{:S(2)}) collective-permute-start(bf16[64,2048]{1,0:T(8,128)(2,1)S(1)} %fusion.84), channel_id=1, source_target_pairs={{0,14},{2,0},{4,2},{6,4},{8,6},{10,8},{12,10},{14,12},{1,15},{3,1}... | collective-permute-start | bytes 786440 | tf_op jit(solution)/shard_map/ppermute | solution.py:19
  (46 other events, 302.2 us)

commit v2 on v1

--- a/solution.py
+++ b/solution.py
@@ -1,6 +1,10 @@
+import functools
+
 import jax
 import jax.numpy as jnp
 from jax import lax
+from jax.experimental import pallas as pl
+from jax.experimental.pallas import tpu as pltpu
 from jax.sharding import Mesh
 from jax.sharding import PartitionSpec as P
 
@@ -19,16 +23,19 @@
     return lax.ppermute(block, RING, [(i, (i + step) % count) for i in range(count)])
 
 
-def gather_ring(own):
-    half = own.shape[0] // 2
+def gather_near(own):
     blocks = {0: own}
-    for distance in (1, 2, 3):
+    for distance in (1, 2):
         blocks[-distance] = step_ring(blocks[1 - distance], 1)
         blocks[distance] = step_ring(blocks[distance - 1], -1)
-    blocks[4] = jnp.concatenate(
-        (step_ring(blocks[-3][:half], 1), step_ring(blocks[3][half:], -1)), axis=0
-    )
     return blocks
+
+
+def gather_far(blocks):
+    half = blocks[0].shape[0] // 2
+    up, down = step_ring(blocks[-2], 1), step_ring(blocks[2], -1)
+    last = jnp.concatenate((step_ring(up[:half], 1), step_ring(down[half:], -1)), axis=0)
+    return {**blocks, -3: up, 3: down, 4: last}
 
 
 def sum_ring(parts):
@@ -97,31 +104,65 @@
     )
 
 
-def expert_forward(row_block, w_gate, w_up, w_down):
-    gate_part = jnp.dot(row_block, w_gate, preferred_element_type=jnp.float32)
-    up_part = jnp.dot(row_block, w_up, preferred_element_type=jnp.float32)
-    hidden = (gate_part * jax.nn.sigmoid(gate_part) * up_part).astype(jnp.bfloat16)
-    return jnp.dot(hidden, w_down, preferred_element_type=jnp.float32).astype(jnp.bfloat16)
-
-
-def expert_backward(row_block, grad_block, w_gate, w_up, w_down):
-    gate_part = jnp.dot(row_block, w_gate, preferred_element_type=jnp.float32)
-    up_part = jnp.dot(row_block, w_up, preferred_element_type=jnp.float32)
-    sigmoid_part = jax.nn.sigmoid(gate_part)
-    activated = gate_part * sigmoid_part
-    slope = sigmoid_part * (1.0 + gate_part * (1.0 - sigmoid_part))
-    hidden_grad = transposed(grad_block, w_down)
-    gate_grad = (hidden_grad * up_part * slope).astype(jnp.bfloat16)
-    up_grad = (hidden_grad * activated).astype(jnp.bfloat16)
-    return (transposed(gate_grad, w_gate) + transposed(up_grad, w_up)).astype(jnp.bfloat16)
-
-
-def apply_expert(forward_flag, rows, grads, weights):
-    return lax.cond(
-        forward_flag,
-        lambda: expert_forward(rows, *weights),
-        lambda: expert_backward(rows, grads, *weights),
-    )
+def expert_kernel(forward_from, flag, first, second, w_gate, w_up, w_down, out, total):
+    step = pl.program_id(0)
+    forward = flag[0] == 1
+
+    @pl.when(step == 0)
+    def _():
+        total[...] = jnp.zeros_like(total)
+
+    @pl.when(forward)
+    def _():
+        rows = (first, second)[forward_from][...]
+        gate_part = jnp.dot(rows, w_gate[...], preferred_element_type=jnp.float32)
+        up_part = jnp.dot(rows, w_up[...], preferred_element_type=jnp.float32)
+        hidden = (gate_part * jax.nn.sigmoid(gate_part) * up_part).astype(jnp.bfloat16)
+        total[...] += jnp.dot(hidden, w_down[...], preferred_element_type=jnp.float32)
+
+    @pl.when(jnp.logical_not(forward))
+    def _():
+        rows = first[...]
+        gate_part = jnp.dot(rows, w_gate[...], preferred_element_type=jnp.float32)
+        up_part = jnp.dot(rows, w_up[...], preferred_element_type=jnp.float32)
+        hidden_grad = transposed(second[...], w_down[...])
+        sigmoid_part = jax.nn.sigmoid(gate_part)
+        activated = gate_part * sigmoid_part
+        slope = sigmoid_part * (1.0 + gate_part * (1.0 - sigmoid_part))
+        gate_grad = (hidden_grad * up_part * slope).astype(jnp.bfloat16)
+        up_grad = (hidden_grad * activated).astype(jnp.bfloat16)
+        total[...] += transposed(gate_grad, w_gate[...]) + transposed(up_grad, w_up[...])
+
+    @pl.when(step == pl.num_programs(0) - 1)
+    def _():
+        out[...] = total[...].astype(jnp.bfloat16)
+
+
+def apply_expert(flag, first, first_at, second, second_at, forward_from, weights):
+    rows, width = first.shape[0], weights[0].shape[0]
+    inner = weights[0].shape[1]
+    depth = inner // 3
+    return pl.pallas_call(
+        functools.partial(expert_kernel, forward_from),
+        grid=(inner // depth,),
+        in_specs=[
+            pl.BlockSpec(memory_space=pltpu.SMEM),
+            pl.BlockSpec((rows, width), lambda j: (0, first_at)),
+            pl.BlockSpec((rows, width), lambda j: (0, second_at)),
+            pl.BlockSpec((width, depth), lambda j: (0, j)),
+            pl.BlockSpec((width, depth), lambda j: (0, j)),
+            pl.BlockSpec((depth, width), lambda j: (j, 0)),
+        ],
+        out_specs=pl.BlockSpec((rows, width), lambda j: (0, 0)),
+        out_shape=jax.ShapeDtypeStruct((rows, width), jnp.bfloat16),
+        scratch_shapes=[pltpu.VMEM((rows, width), jnp.float32)],
+        cost_estimate=pl.CostEstimate(
+            flops=10 * rows * width * inner,
+            bytes_accessed=6 * width * (rows + inner),
+            transcendentals=rows * inner,
+        ),
+        compiler_params=pltpu.CompilerParams(vmem_limit_bytes=48 * 1024 * 1024),
+    )(flag, first, second, *weights)
 
 
 def finish(widened, scaling, gain_row, upstream, summed, forward_flag):
@@ -137,10 +178,18 @@
     return jnp.concatenate([blocks[k] for k in chunk], axis=0)
 
 
+def after(first, then):
+    return lax.optimization_barrier((first, then))
+
+
 def returned(outcomes, weighings, code_sum):
+    near, far = outcomes
+    far_back = exchange(far)
+    far_back, near = after(far_back, near)
+    near_back = exchange(near)
     parts = {}
-    for chunk, outcome, weighing in reversed(list(zip(CHUNKS, outcomes, weighings))):
-        share = combine(weighing, exchange(outcome)).reshape(len(chunk), -1, outcome.shape[-1])
+    for chunk, back, weighing in zip(CHUNKS, (near_back, far_back), weighings):
+        share = combine(weighing, back).reshape(len(chunk), -1, back.shape[-1])
         for i, k in enumerate(chunk):
             parts[k] = share[i]
     return sum_ring(parts) / code_sum
@@ -169,36 +218,51 @@
     stored_normed = normalize(stored, gain_row)[2]
     early_rows = jnp.where(first_segment, stored_normed, edge_rows)
 
-    blocks = gather_ring(jnp.concatenate((normed, info), axis=1))
-    early_blocks = gather_ring(early_rows)
-    arrived_rows, kept_rows, place_next, weigh_now, weigh_next = [], [], [], [], []
+    forward_first = first_segment.astype(jnp.int32).reshape(1)
+
+    blocks = gather_near(jnp.concatenate((normed, early_rows, info), axis=1))
+    pairs, place_next, weigh_now, weigh_next = [], [], [], []
     for chunk in CHUNKS:
+        if pairs:
+            blocks = gather_far(blocks)
         tokens = stack(blocks, chunk)
-        told = jnp.transpose(tokens[:, width : width + 4 * top]).astype(jnp.float32)
+        told = jnp.transpose(tokens[:, 2 * width : 2 * width + 4 * top]).astype(jnp.float32)
         pick_now, by_now = slots(told[:top], told[top : 2 * top])
         pick_next, by_next = slots(told[2 * top : 3 * top], told[3 * top :])
         pick_early = jnp.where(first_segment, pick_next, pick_now)
-        arrived_rows.append(exchange(pick(pick_now, tokens[:, :width])))
-        kept_rows.append(exchange(pick(pick_early, stack(early_blocks, chunk))))
+        picked = jnp.concatenate(
+            (
+                pick(pick_now, tokens[:, :width]),
+                pick(pick_early, tokens[:, width : 2 * width]),
+            ),
+            axis=1,
+        )
+        if pairs:
+            pairs[-1], picked = after(pairs[-1], picked)
+        else:
+            picked, blocks = after(picked, blocks)
+        pairs.append(exchange(picked))
         place_next.append(pick_next)
         weigh_now.append(by_now)
         weigh_next.append(by_next)
-    outcomes = [
-        apply_expert(first_segment, rows, grads, weights)
-        for rows, grads in zip(arrived_rows, kept_rows)
-    ]
+    outcomes = [apply_expert(forward_first, pair, 0, pair, 1, 0, weights) for pair in pairs]
     summed = returned(outcomes, weigh_now, sum_now)
     produced = finish(widened, scaling, gain_row, edge_rows, summed, first_segment)
 
     arrived = lax.ppermute(produced, "segment", [(0, 1), (1, 0)])
     inputs_next = jnp.where(first_segment, stored, arrived)
     widened_next, scaling_next, normed_next = normalize(inputs_next, gain_row)
-    member_blocks = gather_ring(jnp.where(first_segment, arrived, normed_next))
-    outcomes = []
+    member_blocks = gather_far(gather_near(jnp.where(first_segment, arrived, normed_next)))
+    landed = []
     for i, chunk in enumerate(CHUNKS):
-        landed = exchange(pick(place_next[i], stack(member_blocks, chunk)))
-        rows = jnp.where(first_segment, kept_rows[i], landed)
-        outcomes.append(apply_expert(later_forward, rows, landed, weights))
+        picked = pick(place_next[i], stack(member_blocks, chunk))
+        if landed:
+            landed[-1], picked = after(landed[-1], picked)
+        landed.append(exchange(picked))
+    outcomes = [
+        apply_expert(1 - forward_first, pair, 1, rows, 0, 1, weights)
+        for pair, rows in zip(pairs, landed)
+    ]
     summed = returned(outcomes, weigh_next, sum_next)
     result = finish(widened_next, scaling_next, gain_row, arrived, summed, later_forward)
     return result[None]

time: 508 us -> 426 us (0.84)
  matrix products: 95.3 us -> 23.5 us
  Pallas kernels: 0 us -> 47.2 us
  waiting for transfers between devices: 254 us -> 213 us
  starting transfers between devices: 111 us -> 91.7 us
    dot_general x12 -> x0, matrix products: 69.2 us -> none  [the longest x6 33.9 us: transposed(): lax.dot_general(left, right, (((1,), (1,)), ((), ())), preferred_element_...]
    all_to_all x10 -> x8, waiting for transfers between devices: 174 us -> 117 us  [exchange(): lax.all_to_all(parts, PLANE, split_axis=0, concat_axis=0, tiled=True)]
    pallas_call x0 -> x4, Pallas kernels: none -> 47.2 us  [apply_expert(): pl.pallas_call(functools.partial(expert_kernel, forward_from), grid=(inne...]
    ppermute x40 -> x32, waiting for transfers between devices: 75.7 us -> 91.9 us  [step_ring(): lax.ppermute(block, RING, [(i, (i + step) % count) for i in range(count)])]
    all_to_all x10 -> x8, starting transfers between devices: 42.9 us -> 35.4 us  [exchange(): lax.all_to_all(parts, PLANE, split_axis=0, concat_axis=0, tiled=True)]
    ppermute x40 -> x32, starting transfers between devices: 55.8 us -> 48.7 us  [step_ring(): lax.ppermute(block, RING, [(i, (i + step) % count) for i in range(count)])]
    unnamed x124 -> x80, local copies, waits for them, and re-layouts: 10.1 us -> 10.8 us
  transfers between devices with their start and end apart: 51 -> 41, of which waited for: 31 -> 26; matrix products, arithmetic and copies ran while one was open for 17% -> 10% of each run, Pallas kernels for 0% -> 6%
where the time goes in v2:
time: 426 us; the launch traced here: 417 us
  waiting for transfers between devices  213 us (50%)
  starting transfers between devices  91.7 us (22%)
  Pallas kernels  47.2 us (11%)
  matrix products  23.5 us (6%)
  other arithmetic  22.2 us (5%)
  local copies, waits for them, and re-layouts  17.9 us (4%)
    all_to_all x8, waiting for transfers between devices, exchange(): lax.all_to_all(parts, PLANE, split_axis=0, concat_axis=0, tiled=True)  117 us
    ppermute x32, waiting for transfers between devices, step_ring(): lax.ppermute(block, RING, [(i, (i + step) % count) for i in range(count)])  91.9 us
    ppermute x32, starting transfers between devices, step_ring(): lax.ppermute(block, RING, [(i, (i + step) % count) for i in range(count)])  48.7 us
    pallas_call x4, Pallas kernels, apply_expert(): pl.pallas_call(functools.partial(expert_kernel, forward_from), grid=(inne...  47.2 us
    all_to_all x8, starting transfers between devices, exchange(): lax.all_to_all(parts, PLANE, split_axis=0, concat_axis=0, tiled=True)  35.4 us
    dot_general x6, matrix products, pick(): jnp.dot(picking, tokens, preferred_element_type=jnp.float32)  11.3 us
    unnamed x80, local copies, waits for them, and re-layouts  10.8 us
    dot_general x4, matrix products, combine(): lax.dot_general(weighing, rows, (((0,), (0,)), ((), ())), preferred_eleme...  9.54 us
  transfers between devices with their start and end apart: 41, of which 26 were waited for; matrix products, arithmetic and copies ran while one was open for 10% of the time, Pallas kernels for 6%

profile of v2, /device:TPU:96, one launch (start us, length us, event | category | flops | bytes accessed | tf_op | source)
XLA Modules:
  0.0 417.2 jit_solution(2962848678051003707)
XLA Ops:
  5.9 3.2 collective-permute-start
  9.1 11.5 %collective-permute-done = bf16[64,4224]{1,0:T(8,128)(2,1)S(1)} collective-permute-done((bf16[64,4224]{1,0:T(8,128)(2,1)S(1)}, bf16[64,4224]{1,0:T(8,128)(2,1)S(1)}, u32[]{:S(2)}, u32[]{:S(2)}) %collective-permute-start) | collective-permute-done | bytes 540704 | tf_op jit(solution)/shard_map/ppermute | solution.py:23
  20.7 3.7 collective-permute-start.2
  25.2 9.8 %collective-permute-done.2 = bf16[64,4224]{1,0:T(8,128)(2,1)} collective-permute-done((bf16[64,4224]{1,0:T(8,128)(2,1)S(1)}, bf16[64,4224]{1,0:T(8,128)(2,1)}, u32[]{:S(2)}, u32[]{:S(2)}) %collective-permute-start.2) | collective-permute-done | bytes 540704 | tf_op jit(solution)/shard_map/ppermute | solution.py:23
  37.9 1.6 convolution_convert_fusion.4
  41.0 2.0 pad_maximum_fusion
  43.0 3.8 collective-permute-start.4
  46.8 7.0 %all-to-all-start = ((bf16[16,24,4096]{2,1,0:T(8,128)(2,1)}), bf16[16,24,4096]{2,1,0:T(8,128)(2,1)S(1)}, u32[]{:S(2)}, u32[]{:S(2)}) async-start(bf16[16,24,4096]{2,1,0:T(8,128)(2,1)} %bitcast.103), calls=%async_computation | async-start | bytes 6291456 | tf_op jit(solution)/shard_map/all_to_all | solution.py:58
  54.9 1.9 collective-permute-done.4
  57.8 3.8 collective-permute-start.6
  65.6 4.9 %collective-permute-done.7 = bf16[32,4224]{1,0:T(8,128)(2,1)S(1)} collective-permute-done((bf16[32,4224]{1,0:T(8,128)(2,1)S(1)}, bf16[32,4224]{1,0:T(8,128)(2,1)S(1)}, u32[]{:S(2)}, u32[]{:S(2)}) %collective-permute-start.7) | collective-permute-done | bytes 270368 | tf_op jit(solution)/shard_map/ppermute | solution.py:23
  80.5 1.8 convolution_convert_fusion.3
  82.3 1.8 convolution_convert_fusion.2
  84.1 2.1 pad_maximum_fusion.1
  86.2 8.3 %all-to-all-done = bf16[16,24,4096]{2,1,0:T(8,128)(2,1)S(1)} async-done(((bf16[16,24,4096]{2,1,0:T(8,128)(2,1)}), bf16[16,24,4096]{2,1,0:T(8,128)(2,1)S(1)}, u32[]{:S(2)}, u32[]{:S(2)}) %all-to-all-start) | async-done | bytes 3145760 | tf_op jit(solution)/shard_map/all_to_all | solution.py:58
  94.4 4.5 %all-to-all-start.1 = ((bf16[16,24,4096]{2,1,0:T(8,128)(2,1)}), bf16[16,24,4096]{2,1,0:T(8,128)(2,1)}, u32[]{:S(2)}, u32[]{:S(2)}) async-start(bf16[16,24,4096]{2,1,0:T(8,128)(2,1)} %bitcast.104), calls=%async_computation.1 | async-start | bytes 6291456 | tf_op jit(solution)/shard_map/all_to_all | solution.py:58
  98.9 40.6 %all-to-all-done.1 = bf16[16,24,4096]{2,1,0:T(8,128)(2,1)} async-done(((bf16[16,24,4096]{2,1,0:T(8,128)(2,1)}), bf16[16,24,4096]{2,1,0:T(8,128)(2,1)}, u32[]{:S(2)}, u32[]{:S(2)}) %all-to-all-start.1) | async-done | bytes 3145760 | tf_op jit(solution)/shard_map/all_to_all | solution.py:58
  139.5 8.4 %shard_map.82 = bf16[384,2048]{1,0:T(8,128)(2,1)S(1)} custom-call(s32[1]{0:T(128)} %bitcast.8.flag, bf16[384,4096]{1,0:T(8,128)(2,1)} %bitcast.17.first.second, bf16[384,4096]{1,0:T(8,128)(2,1)} %bitcast.17.first.second, bf16[2048,768]{1,0:T(8,128)(2,1)} %bitcast.114, bf16[2048,768]{1,0:T(8,128)(2,1)} %bitcast.118, bf16[768,2048]{1,0:T(8,128)(2,1)} %bitcast.122), custom_call_target="tpu_custom_call" | custom-call | flops 6039797760 | bytes 14155776 | tf_op jit(solution)/shard_map/pallas_call | solution.py:145
  149.2 4.8 %all-to-all-start.2 = ((bf16[16,24,2048]{2,1,0:T(8,128)(2,1)}), bf16[16,24,2048]{2,1,0:T(8,128)(2,1)}, u32[]{:S(2)}, u32[]{:S(2)}) async-start(bf16[16,24,2048]{2,1,0:T(8,128)(2,1)} %bitcast.102), calls=%async_computation.2 | async-start | bytes 3145728 | tf_op jit(solution)/shard_map/all_to_all | solution.py:58
  154.0 8.2 %shard_map.83 = bf16[384,2048]{1,0:T(8,128)(2,1)} custom-call(s32[1]{0:T(128)} %bitcast.8.flag, bf16[384,4096]{1,0:T(8,128)(2,1)S(1)} %bitcast.96, bf16[384,4096]{1,0:T(8,128)(2,1)S(1)} %bitcast.97, bf16[2048,768]{1,0:T(8,128)(2,1)} %bitcast.115, bf16[2048,768]{1,0:T(8,128)(2,1)} %bitcast.119, bf16[768,2048]{1,0:T(8,128)(2,1)} %bitcast.123), custom_call_target="tpu_custom_call" | custom-call | flops 6039797760 | bytes 14155776 | tf_op jit(solution)/shard_map/pallas_call | solution.py:145
  162.2 15.4 %all-to-all-done.2 = bf16[16,24,2048]{2,1,0:T(8,128)(2,1)} async-done(((bf16[16,24,2048]{2,1,0:T(8,128)(2,1)}), bf16[16,24,2048]{2,1,0:T(8,128)(2,1)}, u32[]{:S(2)}, u32[]{:S(2)}) %all-to-all-start.2) | async-done | bytes 1572896 | tf_op jit(solution)/shard_map/all_to_all | solution.py:58
  177.7 3.5 fusion.123
  181.3 3.3 collective-permute-start.8
  184.6 3.7 all-to-all-start.3
  189.5 2.5 collective-permute-start.9
  192.1 6.0 %collective-permute-done.9 = bf16[64,2048]{1,0:T(8,128)(2,1)S(1)} collective-permute-done((bf16[64,2048]{1,0:T(8,128)(2,1)S(1)}, bf16[64,2048]{1,0:T(8,128)(2,1)S(1)}, u32[]{:S(2)}, u32[]{:S(2)}) %collective-permute-start.9) | collective-permute-done | bytes 262176 | tf_op jit(solution)/shard_map/ppermute | solution.py:23
  199.2 3.2 collective-permute-start.10
  202.4 9.6 %all-to-all-done.3 = bf16[16,24,2048]{2,1,0:T(8,128)(2,1)S(1)} async-done(((bf16[16,24,2048]{2,1,0:T(8,128)(2,1)}), bf16[16,24,2048]{2,1,0:T(8,128)(2,1)S(1)}, u32[]{:S(2)}, u32[]{:S(2)}) %all-to-all-start.3) | async-done | bytes 1572896 | tf_op jit(solution)/shard_map/all_to_all | solution.py:58
  213.1 3.2 collective-permute-start.11
  216.3 5.8 %collective-permute-done.14 = bf16[64,2048]{1,0:T(8,128)(2,1)S(1)} collective-permute-done((bf16[64,2048]{1,0:T(8,128)(2,1)S(1)}, bf16[64,2048]{1,0:T(8,128)(2,1)S(1)}, u32[]{:S(2)}, u32[]{:S(2)}) %collective-permute-start.14) | collective-permute-done | bytes 262176 | tf_op jit(solution)/shard_map/ppermute | solution.py:23
  222.6 7.9 %collective-permute-done.15 = bf16[64,2048]{1,0:T(8,128)(2,1)S(1)} collective-permute-done((bf16[64,2048]{1,0:T(8,128)(2,1)S(1)}, bf16[64,2048]{1,0:T(8,128)(2,1)S(1)}, u32[]{:S(2)}, u32[]{:S(2)}) %collective-permute-start.15) | collective-permute-done | bytes 262176 | tf_op jit(solution)/shard_map/ppermute | solution.py:23
  231.2 7.6 %collective-permute-start.16 = (bf16[64,2048]{1,0:T(8,128)(2,1)S(1)}, bf16[64,2048]{1,0:T(8,128)(2,1)S(1)}, u32[]{:S(2)}, u32[]{:S(2)}) collective-permute-start(bf16[64,2048]{1,0:T(8,128)(2,1)S(1)} %fusion.32), channel_id=1, source_target_pairs={{0,128},{128,0},{1,129},{129,1},{2,130},{130,2},{3,131},{131,3},{4... | collective-permute-start | bytes 786440 | tf_op jit(solution)/shard_map/ppermute | solution.py:252
  238.9 4.4 %collective-permute-done.16 = bf16[64,2048]{1,0:T(8,128)(2,1)S(1)} collective-permute-done((bf16[64,2048]{1,0:T(8,128)(2,1)S(1)}, bf16[64,2048]{1,0:T(8,128)(2,1)S(1)}, u32[]{:S(2)}, u32[]{:S(2)}) %collective-permute-start.16) | collective-permute-done | bytes 262176 | tf_op jit(solution)/shard_map/ppermute | solution.py:252
  244.2 2.0 collective-permute-start.18
  246.2 6.0 %collective-permute-done.17 = bf16[64,2048]{1,0:T(8,128)(2,1)S(1)} collective-permute-done((bf16[64,2048]{1,0:T(8,128)(2,1)S(1)}, bf16[64,2048]{1,0:T(8,128)(2,1)S(1)}, u32[]{:S(2)}, u32[]{:S(2)}) %collective-permute-start.17) | collective-permute-done | bytes 262176 | tf_op jit(solution)/shard_map/ppermute | solution.py:23
  252.2 2.0 collective-permute-start.20
  254.2 4.4 %collective-permute-done.19 = bf16[64,2048]{1,0:T(8,128)(2,1)} collective-permute-done((bf16[64,2048]{1,0:T(8,128)(2,1)S(1)}, bf16[64,2048]{1,0:T(8,128)(2,1)}, u32[]{:S(2)}, u32[]{:S(2)}) %collective-permute-start.19) | collective-permute-done | bytes 262176 | tf_op jit(solution)/shard_map/ppermute | solution.py:23
  258.7 2.8 convolution_convert_fusion.1
  261.5 4.0 all-to-all-start.4
  265.5 2.0 collective-permute-start.21
  268.6 5.7 %collective-permute-done.21 = bf16[64,2048]{1,0:T(8,128)(2,1)S(1)} collective-permute-done((bf16[64,2048]{1,0:T(8,128)(2,1)}, bf16[64,2048]{1,0:T(8,128)(2,1)S(1)}, u32[]{:S(2)}, u32[]{:S(2)}) %collective-permute-start.21) | collective-permute-done | bytes 262176 | tf_op jit(solution)/shard_map/ppermute | solution.py:23
  274.3 3.2 collective-permute-start.23
  277.7 2.4 collective-permute-done.23
  280.1 3.7 collective-permute-done.24
  283.8 1.8 convolution_convert_fusion
  285.6 3.6 all-to-all-done.4
  289.2 3.9 all-to-all-start.5
  293.1 23.6 %all-to-all-done.5 = bf16[16,24,2048]{2,1,0:T(8,128)(2,1)S(1)} async-done(((bf16[16,24,2048]{2,1,0:T(8,128)(2,1)}), bf16[16,24,2048]{2,1,0:T(8,128)(2,1)S(1)}, u32[]{:S(2)}, u32[]{:S(2)}) %all-to-all-start.5) | async-done | bytes 1572896 | tf_op jit(solution)/shard_map/all_to_all | solution.py:58
  316.8 14.7 %shard_map.84 = bf16[384,2048]{1,0:T(8,128)(2,1)S(1)} custom-call(s32[1]{0:T(128)S(6)} %sub.66.flag, bf16[384,4096]{1,0:T(8,128)(2,1)} %bitcast.17.first.second, bf16[384,2048]{1,0:T(8,128)(2,1)S(1)} %bitcast.100, bf16[2048,768]{1,0:T(8,128)(2,1)} %bitcast.116, bf16[2048,768]{1,0:T(8,128)(2,1)} %bitcast.120, bf16[768,2048]{1,0:T(8,128)(2,1)} %bitcast.124), custom_call_target="tpu_custom_call" | custom-call | flops 6039797760 | bytes 14155776 | tf_op jit(solution)/shard_map/pallas_call | solution.py:145
  332.7 3.7 all-to-all-start.6
  336.4 15.9 %shard_map.85 = bf16[384,2048]{1,0:T(8,128)(2,1)} custom-call(s32[1]{0:T(128)S(6)} %sub.66.flag, bf16[384,4096]{1,0:T(8,128)(2,1)} %bitcast.98, bf16[384,2048]{1,0:T(8,128)(2,1)S(1)} %bitcast.99, bf16[2048,768]{1,0:T(8,128)(2,1)} %bitcast.117, bf16[2048,768]{1,0:T(8,128)(2,1)} %bitcast.121, bf16[768,2048]{1,0:T(8,128)(2,1)} %bitcast.125), custom_call_target="tpu_custom_call" | custom-call | flops 6039797760 | bytes 14155776 | tf_op jit(solution)/shard_map/pallas_call | solution.py:145
  352.3 7.8 %all-to-all-done.6 = bf16[16,24,2048]{2,1,0:T(8,128)(2,1)S(1)} async-done(((bf16[16,24,2048]{2,1,0:T(8,128)(2,1)}), bf16[16,24,2048]{2,1,0:T(8,128)(2,1)S(1)}, u32[]{:S(2)}, u32[]{:S(2)}) %all-to-all-start.6) | async-done | bytes 1572896 | tf_op jit(solution)/shard_map/all_to_all | solution.py:58
  360.0 3.0 fusion.124
  363.1 2.0 collective-permute-start.25
  365.2 3.7 all-to-all-start.7
  368.9 2.3 collective-permute-done.29
  374.8 4.7 %collective-permute-done.26 = bf16[64,2048]{1,0:T(8,128)(2,1)S(1)} collective-permute-done((bf16[64,2048]{1,0:T(8,128)(2,1)S(1)}, bf16[64,2048]{1,0:T(8,128)(2,1)S(1)}, u32[]{:S(2)}, u32[]{:S(2)}) %collective-permute-start.26) | collective-permute-done | bytes 262176 | tf_op jit(solution)/shard_map/ppermute | solution.py:23
  380.6 3.8 collective-permute-start.27
  384.4 8.2 %all-to-all-done.7 = bf16[16,24,2048]{2,1,0:T(8,128)(2,1)S(1)} async-done(((bf16[16,24,2048]{2,1,0:T(8,128)(2,1)}), bf16[16,24,2048]{2,1,0:T(8,128)(2,1)S(1)}, u32[]{:S(2)}, u32[]{:S(2)}) %all-to-all-start.7) | async-done | bytes 1572896 | tf_op jit(solution)/shard_map/all_to_all | solution.py:58
  393.8 2.2 convolution_bitcast_fusion
  396.0 1.8 fusion.47
  397.8 3.2 collective-permute-start.28
  401.0 5.9 %collective-permute-done.31 = bf16[64,2048]{1,0:T(8,128)(2,1)S(1)} collective-permute-done((bf16[64,2048]{1,0:T(8,128)(2,1)S(1)}, bf16[64,2048]{1,0:T(8,128)(2,1)S(1)}, u32[]{:S(2)}, u32[]{:S(2)}) %collective-permute-start.31) | collective-permute-done | bytes 262176 | tf_op jit(solution)/shard_map/ppermute | solution.py:23
  407.1 8.3 %collective-permute-done.32 = bf16[64,2048]{1,0:T(8,128)(2,1)S(1)} collective-permute-done((bf16[64,2048]{1,0:T(8,128)(2,1)S(1)}, bf16[64,2048]{1,0:T(8,128)(2,1)S(1)}, u32[]{:S(2)}, u32[]{:S(2)}) %collective-permute-start.32) | collective-permute-done | bytes 262176 | tf_op jit(solution)/shard_map/ppermute | solution.py:23
  (181 shorter events, 43.7 us)
Async XLA Ops:
  0.8 5.0 %copy-start.12 = (s32[1,1,64,8]{3,2,1,0:T(8,128)}, s32[1,1,64,8]{3,2,1,0:T(8,128)S(1)}, u32[]{:S(2)}) copy-start(s32[1,1,64,8]{3,2,1,0:T(8,128)S(1)} %copy.35) | copy-start | bytes 6148
  5.9 14.7 %collective-permute-start = (bf16[64,4224]{1,0:T(8,128)(2,1)S(1)}, bf16[64,4224]{1,0:T(8,128)(2,1)S(1)}, u32[]{:S(2)}, u32[]{:S(2)}) collective-permute-start(bf16[64,4224]{1,0:T(8,128)(2,1)S(1)} %pad_maximum_fusion.12), channel_id=1, source_target_pairs={{0,2},{2,4},{4,6},{6,8},{8,10},{10,12},{12,14},{14,0},{1,3},{3,5},... | collective-permute-start | bytes 1622024 | tf_op jit(solution)/shard_map/ppermute | solution.py:23
  9.1 16.0 %collective-permute-start.1 = (bf16[64,4224]{1,0:T(8,128)(2,1)S(1)}, bf16[64,4224]{1,0:T(8,128)(2,1)S(1)}, u32[]{:S(2)}, u32[]{:S(2)}) collective-permute-start(bf16[64,4224]{1,0:T(8,128)(2,1)S(1)} %pad_maximum_fusion.12), channel_id=1, source_target_pairs={{0,14},{2,0},{4,2},{6,4},{8,6},{10,8},{12,10},{14,12},{1,15},{3,1}... | collective-permute-start | bytes 1622024 | tf_op jit(solution)/shard_map/ppermute | solution.py:23
  20.7 14.4 %collective-permute-start.2 = (bf16[64,4224]{1,0:T(8,128)(2,1)S(1)}, bf16[64,4224]{1,0:T(8,128)(2,1)}, u32[]{:S(2)}, u32[]{:S(2)}) collective-permute-start(bf16[64,4224]{1,0:T(8,128)(2,1)S(1)} %collective-permute-done), channel_id=1, source_target_pairs={{0,2},{2,4},{4,6},{6,8},{8,10},{10,12},{12,14},{14,0},{1,3},{3,5},... | collective-permute-start | bytes 1622024 | tf_op jit(solution)/shard_map/ppermute | solution.py:23
  25.0 12.7 %copy-start.20 = (f32[384]{0:T(512)}, f32[384]{0:T(512)S(1)}, u32[]{:S(2)}) copy-start(f32[384]{0:T(512)S(1)} %eq.170) | copy-start | bytes 4612
  25.0 12.3 %copy-start.33 = (pred[256]{0:T(512)(128)(4,1)}, pred[256]{0:T(512)(128)(4,1)S(1)}, u32[]{:S(2)}) copy-start(pred[256]{0:T(512)(128)(4,1)S(1)} %compare_and_fusion) | copy-start | bytes 772
  25.0 12.3 %copy-start.28 = (f32[16]{0:T(128)}, f32[16]{0:T(128)S(1)}, u32[]{:S(2)}) copy-start(f32[16]{0:T(128)S(1)} %fusion.104) | copy-start | bytes 196
  25.1 12.3 %copy-start.32 = (s32[256]{0:T(256)}, s32[256]{0:T(256)S(1)}, u32[]{:S(2)}) copy-start(s32[256]{0:T(256)S(1)} %fusion.102) | copy-start | bytes 3076
  25.1 12.3 %copy-start.30 = (s32[256]{0:T(256)}, s32[256]{0:T(256)S(1)}, u32[]{:S(2)}) copy-start(s32[256]{0:T(256)S(1)} %get-tuple-element.94) | copy-start | bytes 3076
  25.1 12.3 %copy-start.31 = (f32[256]{0:T(256)}, f32[256]{0:T(256)S(1)}, u32[]{:S(2)}) copy-start(f32[256]{0:T(256)S(1)} %get-tuple-element.95) | copy-start | bytes 3076
  25.1 17.9 %collective-permute-start.3 = (bf16[64,4224]{1,0:T(8,128)(2,1)S(1)}, bf16[64,4224]{1,0:T(8,128)(2,1)}, u32[]{:S(2)}, u32[]{:S(2)}) collective-permute-start(bf16[64,4224]{1,0:T(8,128)(2,1)S(1)} %collective-permute-done.1), channel_id=1, source_target_pairs={{0,14},{2,0},{4,2},{6,4},{8,6},{10,8},{12,10},{14,12},{1,15},{3,1}... | collective-permute-start | bytes 1622024 | tf_op jit(solution)/shard_map/ppermute | solution.py:23
  43.0 13.8 %collective-permute-start.4 = (bf16[64,4224]{1,0:T(8,128)(2,1)}, bf16[64,4224]{1,0:T(8,128)(2,1)}, u32[]{:S(2)}, u32[]{:S(2)}) collective-permute-start(bf16[64,4224]{1,0:T(8,128)(2,1)} %collective-permute-done.2), channel_id=1, source_target_pairs={{0,2},{2,4},{4,6},{6,8},{8,10},{10,12},{12,14},{14,0},{1,3},{3,5},... | collective-permute-start | bytes 1622024 | tf_op jit(solution)/shard_map/ppermute | solution.py:23
  46.8 14.8 %collective-permute-start.5 = (bf16[64,4224]{1,0:T(8,128)(2,1)}, bf16[64,4224]{1,0:T(8,128)(2,1)}, u32[]{:S(2)}, u32[]{:S(2)}) collective-permute-start(bf16[64,4224]{1,0:T(8,128)(2,1)} %collective-permute-done.3), channel_id=1, source_target_pairs={{0,14},{2,0},{4,2},{6,4},{8,6},{10,8},{12,10},{14,12},{1,15},{3,1}... | collective-permute-start | bytes 1622024 | tf_op jit(solution)/shard_map/ppermute | solution.py:23
  46.8 47.6 %all-to-all-start = ((bf16[16,24,4096]{2,1,0:T(8,128)(2,1)}), bf16[16,24,4096]{2,1,0:T(8,128)(2,1)S(1)}, u32[]{:S(2)}, u32[]{:S(2)}) async-start(bf16[16,24,4096]{2,1,0:T(8,128)(2,1)} %bitcast.103), calls=%async_computation | async-start | bytes 6291456 | tf_op jit(solution)/shard_map/all_to_all | solution.py:58
  57.8 7.7 %collective-permute-start.6 = (bf16[32,4224]{1,0:T(8,128)(2,1)S(1)}, bf16[32,4224]{1,0:T(8,128)(2,1)S(1)}, u32[]{:S(2)}, u32[]{:S(2)}) collective-permute-start(bf16[32,4224]{1,0:T(8,128)(2,1)S(1)} %slice.231), channel_id=1, source_target_pairs={{0,2},{2,4},{4,6},{6,8},{8,10},{10,12},{12,14},{14,0},{1,3},{3,5},... | collective-permute-start | bytes 811016 | tf_op jit(solution)/shard_map/ppermute | solution.py:23
  62.6 8.0 %collective-permute-start.7 = (bf16[32,4224]{1,0:T(8,128)(2,1)S(1)}, bf16[32,4224]{1,0:T(8,128)(2,1)S(1)}, u32[]{:S(2)}, u32[]{:S(2)}) collective-permute-start(bf16[32,4224]{1,0:T(8,128)(2,1)S(1)} %slice.232), channel_id=1, source_target_pairs={{0,14},{2,0},{4,2},{6,4},{8,6},{10,8},{12,10},{14,12},{1,15},{3,1}... | collective-permute-start | bytes 811016 | tf_op jit(solution)/shard_map/ppermute | solution.py:23
  94.4 59.5 %copy-start = (bf16[16,24,4096]{2,1,0:T(8,128)(2,1)}, bf16[16,24,4096]{2,1,0:T(8,128)(2,1)S(1)}, u32[]{:S(2)}) copy-start(bf16[16,24,4096]{2,1,0:T(8,128)(2,1)S(1)} %all-to-all-done) | copy-start | bytes 9437188
  94.4 45.1 %all-to-all-start.1 = ((bf16[16,24,4096]{2,1,0:T(8,128)(2,1)}), bf16[16,24,4096]{2,1,0:T(8,128)(2,1)}, u32[]{:S(2)}, u32[]{:S(2)}) async-start(bf16[16,24,4096]{2,1,0:T(8,128)(2,1)} %bitcast.104), calls=%async_computation.1 | async-start | bytes 6291456 | tf_op jit(solution)/shard_map/all_to_all | solution.py:58
  149.2 28.5 %all-to-all-start.2 = ((bf16[16,24,2048]{2,1,0:T(8,128)(2,1)}), bf16[16,24,2048]{2,1,0:T(8,128)(2,1)}, u32[]{:S(2)}, u32[]{:S(2)}) async-start(bf16[16,24,2048]{2,1,0:T(8,128)(2,1)} %bitcast.102), calls=%async_computation.2 | async-start | bytes 3145728 | tf_op jit(solution)/shard_map/all_to_all | solution.py:58
  181.2 7.2 %collective-permute-start.12 = (bf16[32,2048]{1,0:T(8,128)(2,1)S(1)}, bf16[32,2048]{1,0:T(8,128)(2,1)S(1)}, u32[]{:S(2)}, u32[]{:S(2)}) collective-permute-start(bf16[32,2048]{1,0:T(8,128)(2,1)S(1)} %get-tuple-element.56), channel_id=1, source_target_pairs={{0,14},{2,0},{4,2},{6,4},{8,6},{10,8},{12,10},{14,12},{1,15},{3,1}... | collective-permute-start | bytes 393224 | tf_op jit(solution)/shard_map/ppermute | solution.py:23
  181.3 7.1 %collective-permute-start.8 = (bf16[32,2048]{1,0:T(8,128)(2,1)S(1)}, bf16[32,2048]{1,0:T(8,128)(2,1)S(1)}, u32[]{:S(2)}, u32[]{:S(2)}) collective-permute-start(bf16[32,2048]{1,0:T(8,128)(2,1)S(1)} %get-tuple-element.55), channel_id=1, source_target_pairs={{0,2},{2,4},{4,6},{6,8},{8,10},{10,12},{12,14},{14,0},{1,3},{3,5},... | collective-permute-start | bytes 393224 | tf_op jit(solution)/shard_map/ppermute | solution.py:23
  184.6 27.4 %all-to-all-start.3 = ((bf16[16,24,2048]{2,1,0:T(8,128)(2,1)}), bf16[16,24,2048]{2,1,0:T(8,128)(2,1)S(1)}, u32[]{:S(2)}, u32[]{:S(2)}) async-start(bf16[16,24,2048]{2,1,0:T(8,128)(2,1)} %bitcast.23), calls=%async_computation.3 | async-start | bytes 3145728 | tf_op jit(solution)/shard_map/all_to_all | solution.py:58
  188.3 23.7 %copy-start.19 = (f32[16,256]{1,0:T(8,128)S(1)}, f32[16,256]{1,0:T(8,128)}, u32[]{:S(2)}) copy-start(f32[16,256]{1,0:T(8,128)} %copy-done.18) | copy-start | bytes 49156
  188.4 23.6 %copy-start.22 = (bf16[16,256]{1,0:T(8,128)(2,1)S(1)}, bf16[16,256]{1,0:T(8,128)(2,1)}, u32[]{:S(2)}) copy-start(bf16[16,256]{1,0:T(8,128)(2,1)} %get-tuple-element.40) | copy-start | bytes 24580
  188.4 23.6 %copy-start.24 = (f32[24]{0:T(128)S(1)}, f32[24]{0:T(128)}, u32[]{:S(2)}) copy-start(f32[24]{0:T(128)} %copy-done.23) | copy-start | bytes 292
  189.5 8.6 %collective-permute-start.9 = (bf16[64,2048]{1,0:T(8,128)(2,1)S(1)}, bf16[64,2048]{1,0:T(8,128)(2,1)S(1)}, u32[]{:S(2)}, u32[]{:S(2)}) collective-permute-start(bf16[64,2048]{1,0:T(8,128)(2,1)S(1)} %pad_maximum_fusion.13), channel_id=1, source_target_pairs={{0,2},{2,4},{4,6},{6,8},{8,10},{10,12},{12,14},{14,0},{1,3},{3,5},... | collective-permute-start | bytes 786440 | tf_op jit(solution)/shard_map/ppermute | solution.py:23
  192.0 20.9 %collective-permute-start.13 = (bf16[64,2048]{1,0:T(8,128)(2,1)S(1)}, bf16[64,2048]{1,0:T(8,128)(2,1)S(1)}, u32[]{:S(2)}, u32[]{:S(2)}) collective-permute-start(bf16[64,2048]{1,0:T(8,128)(2,1)S(1)} %pad_maximum_fusion.14), channel_id=1, source_target_pairs={{0,14},{2,0},{4,2},{6,4},{8,6},{10,8},{12,10},{14,12},{1,15},{3,1}... | collective-permute-start | bytes 786440 | tf_op jit(solution)/shard_map/ppermute | solution.py:23
  199.2 13.7 %collective-permute-start.10 = (bf16[64,2048]{1,0:T(8,128)(2,1)S(1)}, bf16[64,2048]{1,0:T(8,128)(2,1)S(1)}, u32[]{:S(2)}, u32[]{:S(2)}) collective-permute-start(bf16[64,2048]{1,0:T(8,128)(2,1)S(1)} %fusion.52), channel_id=1, source_target_pairs={{0,2},{2,4},{4,6},{6,8},{8,10},{10,12},{12,14},{14,0},{1,3},{3,5},... | collective-permute-start | bytes 786440 | tf_op jit(solution)/shard_map/ppermute | solution.py:23
  212.8 9.6 %copy-start.13 = (s32[1,1,64,8]{3,2,1,0:T(8,128)S(1)}, s32[1,1,64,8]{3,2,1,0:T(8,128)}, u32[]{:S(2)}) copy-start(s32[1,1,64,8]{3,2,1,0:T(8,128)} %copy-done.12) | copy-start | bytes 6148
  212.8 9.6 %copy-start.15 = (s32[1,1,64,8]{3,2,1,0:T(8,128)S(1)}, s32[1,1,64,8]{3,2,1,0:T(8,128)}, u32[]{:S(2)}) copy-start(s32[1,1,64,8]{3,2,1,0:T(8,128)} %copy-done.14) | copy-start | bytes 6148
  212.8 17.7 %copy-start.6 = (bf16[64,2048]{1,0:T(8,128)(2,1)S(1)}, bf16[64,2048]{1,0:T(8,128)(2,1)}, u32[]{:S(2)}) copy-start(bf16[64,2048]{1,0:T(8,128)(2,1)} %copy-done.5) | copy-start | bytes 786436
  212.8 17.7 %copy-start.11 = (f32[1,2048]{1,0:T(1,128)S(1)}, f32[1,2048]{1,0:T(1,128)}, u32[]{:S(2)}) copy-start(f32[1,2048]{1,0:T(1,128)} %param.10) | copy-start | bytes 24580
  212.9 17.9 %copy-start.10 = (bf16[1,64,2048]{2,1,0:T(8,128)(2,1)S(1)}, bf16[1,64,2048]{2,1,0:T(8,128)(2,1)}, u32[]{:S(2)}) copy-start(bf16[1,64,2048]{2,1,0:T(8,128)(2,1)} %param.8) | copy-start | bytes 786436
  212.9 17.9 %copy-start.27 = (f32[64]{0:T(128)S(1)}, f32[64]{0:T(128)}, u32[]{:S(2)}) copy-start(f32[64]{0:T(128)} %copy-done.26) | copy-start | bytes 772
  212.9 17.9 %copy-start.29 = (f32[64]{0:T(128)S(1)}, f32[64]{0:T(128)}, u32[]{:S(2)}) copy-start(f32[64]{0:T(128)} %get-tuple-element.85) | copy-start | bytes 772
  213.0 9.1 %collective-permute-start.14 = (bf16[64,2048]{1,0:T(8,128)(2,1)S(1)}, bf16[64,2048]{1,0:T(8,128)(2,1)S(1)}, u32[]{:S(2)}, u32[]{:S(2)}) collective-permute-start(bf16[64,2048]{1,0:T(8,128)(2,1)S(1)} %get-tuple-element.48), channel_id=1, source_target_pairs={{0,14},{2,0},{4,2},{6,4},{8,6},{10,8},{12,10},{14,12},{1,15},{3,1}... | collective-permute-start | bytes 786440 | tf_op jit(solution)/shard_map/ppermute | solution.py:23
  213.1 30.1 %copy-start.3 = (bf16[1,64,2048]{2,1,0:T(8,128)(2,1)S(1)}, bf16[1,64,2048]{2,1,0:T(8,128)(2,1)}, u32[]{:S(2)}) copy-start(bf16[1,64,2048]{2,1,0:T(8,128)(2,1)} %param.9) | copy-start | bytes 786436
  213.1 9.4 %collective-permute-start.11 = (bf16[64,2048]{1,0:T(8,128)(2,1)S(1)}, bf16[64,2048]{1,0:T(8,128)(2,1)S(1)}, u32[]{:S(2)}, u32[]{:S(2)}) collective-permute-start(bf16[64,2048]{1,0:T(8,128)(2,1)S(1)} %get-tuple-element.47), channel_id=1, source_target_pairs={{0,2},{2,4},{4,6},{6,8},{8,10},{10,12},{12,14},{14,0},{1,3},{3,5},... | collective-permute-start | bytes 786440 | tf_op jit(solution)/shard_map/ppermute | solution.py:23
  222.1 8.3 %collective-permute-start.15 = (bf16[64,2048]{1,0:T(8,128)(2,1)S(1)}, bf16[64,2048]{1,0:T(8,128)(2,1)S(1)}, u32[]{:S(2)}, u32[]{:S(2)}) collective-permute-start(bf16[64,2048]{1,0:T(8,128)(2,1)S(1)} %fusion.51), channel_id=1, source_target_pairs={{0,14},{2,0},{4,2},{6,4},{8,6},{10,8},{12,10},{14,12},{1,15},{3,1}... | collective-permute-start | bytes 786440 | tf_op jit(solution)/shard_map/ppermute | solution.py:23
  230.5 28.2 %copy-start.17 = (pred[384,256]{1,0:T(32,128)(4,1)S(1)}, pred[384,256]{1,0:T(32,128)(4,1)}, u32[]{:S(2)}) copy-start(pred[384,256]{1,0:T(32,128)(4,1)} %copy-done.16) | copy-start | bytes 294916
  231.2 12.0 %collective-permute-start.16 = (bf16[64,2048]{1,0:T(8,128)(2,1)S(1)}, bf16[64,2048]{1,0:T(8,128)(2,1)S(1)}, u32[]{:S(2)}, u32[]{:S(2)}) collective-permute-start(bf16[64,2048]{1,0:T(8,128)(2,1)S(1)} %fusion.32), channel_id=1, source_target_pairs={{0,128},{128,0},{1,129},{129,1},{2,130},{130,2},{3,131},{131,3},{4... | collective-permute-start | bytes 786440 | tf_op jit(solution)/shard_map/ppermute | solution.py:252
  244.1 8.1 %collective-permute-start.17 = (bf16[64,2048]{1,0:T(8,128)(2,1)S(1)}, bf16[64,2048]{1,0:T(8,128)(2,1)S(1)}, u32[]{:S(2)}, u32[]{:S(2)}) collective-permute-start(bf16[64,2048]{1,0:T(8,128)(2,1)S(1)} %fusion.59), channel_id=1, source_target_pairs={{0,2},{2,4},{4,6},{6,8},{8,10},{10,12},{12,14},{14,0},{1,3},{3,5},... | collective-permute-start | bytes 786440 | tf_op jit(solution)/shard_map/ppermute | solution.py:23
  244.2 8.0 %collective-permute-start.18 = (bf16[64,2048]{1,0:T(8,128)(2,1)S(1)}, bf16[64,2048]{1,0:T(8,128)(2,1)S(1)}, u32[]{:S(2)}, u32[]{:S(2)}) collective-permute-start(bf16[64,2048]{1,0:T(8,128)(2,1)S(1)} %fusion.59), channel_id=1, source_target_pairs={{0,14},{2,0},{4,2},{6,4},{8,6},{10,8},{12,10},{14,12},{1,15},{3,1}... | collective-permute-start | bytes 786440 | tf_op jit(solution)/shard_map/ppermute | solution.py:23
  252.2 6.5 %collective-permute-start.19 = (bf16[64,2048]{1,0:T(8,128)(2,1)S(1)}, bf16[64,2048]{1,0:T(8,128)(2,1)}, u32[]{:S(2)}, u32[]{:S(2)}) collective-permute-start(bf16[64,2048]{1,0:T(8,128)(2,1)S(1)} %collective-permute-done.17), channel_id=1, source_target_pairs={{0,2},{2,4},{4,6},{6,8},{8,10},{10,12},{12,14},{14,0},{1,3},{3,5},... | collective-permute-start | bytes 786440 | tf_op jit(solution)/shard_map/ppermute | solution.py:23
  252.2 15.3 %collective-permute-start.20 = (bf16[64,2048]{1,0:T(8,128)(2,1)S(1)}, bf16[64,2048]{1,0:T(8,128)(2,1)}, u32[]{:S(2)}, u32[]{:S(2)}) collective-permute-start(bf16[64,2048]{1,0:T(8,128)(2,1)S(1)} %collective-permute-done.18), channel_id=1, source_target_pairs={{0,14},{2,0},{4,2},{6,4},{8,6},{10,8},{12,10},{14,12},{1,15},{3,1}... | collective-permute-start | bytes 786440 | tf_op jit(solution)/shard_map/ppermute | solution.py:23
  261.5 27.7 %all-to-all-start.4 = ((bf16[16,24,2048]{2,1,0:T(8,128)(2,1)}), bf16[16,24,2048]{2,1,0:T(8,128)(2,1)S(1)}, u32[]{:S(2)}, u32[]{:S(2)}) async-start(bf16[16,24,2048]{2,1,0:T(8,128)(2,1)} %bitcast.26), calls=%async_computation.4 | async-start | bytes 3145728 | tf_op jit(solution)/shard_map/all_to_all | solution.py:58
  265.5 8.8 %collective-permute-start.21 = (bf16[64,2048]{1,0:T(8,128)(2,1)}, bf16[64,2048]{1,0:T(8,128)(2,1)S(1)}, u32[]{:S(2)}, u32[]{:S(2)}) collective-permute-start(bf16[64,2048]{1,0:T(8,128)(2,1)} %collective-permute-done.19), channel_id=1, source_target_pairs={{0,2},{2,4},{4,6},{6,8},{8,10},{10,12},{12,14},{14,0},{1,3},{3,5},... | collective-permute-start | bytes 786440 | tf_op jit(solution)/shard_map/ppermute | solution.py:23
  267.5 10.1 %collective-permute-start.22 = (bf16[64,2048]{1,0:T(8,128)(2,1)}, bf16[64,2048]{1,0:T(8,128)(2,1)S(1)}, u32[]{:S(2)}, u32[]{:S(2)}) collective-permute-start(bf16[64,2048]{1,0:T(8,128)(2,1)} %collective-permute-done.20), channel_id=1, source_target_pairs={{0,14},{2,0},{4,2},{6,4},{8,6},{10,8},{12,10},{14,12},{1,15},{3,1}... | collective-permute-start | bytes 786440 | tf_op jit(solution)/shard_map/ppermute | solution.py:23
  274.3 5.7 %collective-permute-start.23 = (bf16[32,2048]{1,0:T(8,128)(2,1)S(1)}, bf16[32,2048]{1,0:T(8,128)(2,1)S(1)}, u32[]{:S(2)}, u32[]{:S(2)}) collective-permute-start(bf16[32,2048]{1,0:T(8,128)(2,1)S(1)} %slice.251), channel_id=1, source_target_pairs={{0,2},{2,4},{4,6},{6,8},{8,10},{10,12},{12,14},{14,0},{1,3},{3,5},... | collective-permute-start | bytes 393224 | tf_op jit(solution)/shard_map/ppermute | solution.py:23
  277.6 6.3 %collective-permute-start.24 = (bf16[32,2048]{1,0:T(8,128)(2,1)S(1)}, bf16[32,2048]{1,0:T(8,128)(2,1)S(1)}, u32[]{:S(2)}, u32[]{:S(2)}) collective-permute-start(bf16[32,2048]{1,0:T(8,128)(2,1)S(1)} %slice.252), channel_id=1, source_target_pairs={{0,14},{2,0},{4,2},{6,4},{8,6},{10,8},{12,10},{14,12},{1,15},{3,1}... | collective-permute-start | bytes 393224 | tf_op jit(solution)/shard_map/ppermute | solution.py:23
  289.2 27.6 %all-to-all-start.5 = ((bf16[16,24,2048]{2,1,0:T(8,128)(2,1)}), bf16[16,24,2048]{2,1,0:T(8,128)(2,1)S(1)}, u32[]{:S(2)}, u32[]{:S(2)}) async-start(bf16[16,24,2048]{2,1,0:T(8,128)(2,1)} %bitcast.106), calls=%async_computation.5 | async-start | bytes 3145728 | tf_op jit(solution)/shard_map/all_to_all | solution.py:58
  332.7 27.4 %all-to-all-start.6 = ((bf16[16,24,2048]{2,1,0:T(8,128)(2,1)}), bf16[16,24,2048]{2,1,0:T(8,128)(2,1)S(1)}, u32[]{:S(2)}, u32[]{:S(2)}) async-start(bf16[16,24,2048]{2,1,0:T(8,128)(2,1)} %bitcast.101), calls=%async_computation.6 | async-start | bytes 3145728 | tf_op jit(solution)/shard_map/all_to_all | solution.py:58
  363.1 5.8 %collective-permute-start.25 = (bf16[32,2048]{1,0:T(8,128)(2,1)S(1)}, bf16[32,2048]{1,0:T(8,128)(2,1)S(1)}, u32[]{:S(2)}, u32[]{:S(2)}) collective-permute-start(bf16[32,2048]{1,0:T(8,128)(2,1)S(1)} %get-tuple-element.51), channel_id=1, source_target_pairs={{0,2},{2,4},{4,6},{6,8},{8,10},{10,12},{12,14},{14,0},{1,3},{3,5},... | collective-permute-start | bytes 393224 | tf_op jit(solution)/shard_map/ppermute | solution.py:23
  365.1 6.2 %collective-permute-start.29 = (bf16[32,2048]{1,0:T(8,128)(2,1)S(1)}, bf16[32,2048]{1,0:T(8,128)(2,1)S(1)}, u32[]{:S(2)}, u32[]{:S(2)}) collective-permute-start(bf16[32,2048]{1,0:T(8,128)(2,1)S(1)} %get-tuple-element.52), channel_id=1, source_target_pairs={{0,14},{2,0},{4,2},{6,4},{8,6},{10,8},{12,10},{14,12},{1,15},{3,1}... | collective-permute-start | bytes 393224 | tf_op jit(solution)/shard_map/ppermute | solution.py:23
  365.2 27.4 %all-to-all-start.7 = ((bf16[16,24,2048]{2,1,0:T(8,128)(2,1)}), bf16[16,24,2048]{2,1,0:T(8,128)(2,1)S(1)}, u32[]{:S(2)}, u32[]{:S(2)}) async-start(bf16[16,24,2048]{2,1,0:T(8,128)(2,1)} %bitcast.32), calls=%async_computation.7 | async-start | bytes 3145728 | tf_op jit(solution)/shard_map/all_to_all | solution.py:58
  368.9 24.8 %copy-start.21 = (bf16[16,256]{1,0:T(8,128)(2,1)S(1)}, bf16[16,256]{1,0:T(8,128)(2,1)}, u32[]{:S(2)}) copy-start(bf16[16,256]{1,0:T(8,128)(2,1)} %get-tuple-element.31) | copy-start | bytes 24580
  368.9 24.8 %copy-start.25 = (f32[24]{0:T(128)S(1)}, f32[24]{0:T(128)}, u32[]{:S(2)}) copy-start(f32[24]{0:T(128)} %copy-done.23) | copy-start | bytes 292
  372.4 7.2 %collective-permute-start.26 = (bf16[64,2048]{1,0:T(8,128)(2,1)S(1)}, bf16[64,2048]{1,0:T(8,128)(2,1)S(1)}, u32[]{:S(2)}, u32[]{:S(2)}) collective-permute-start(bf16[64,2048]{1,0:T(8,128)(2,1)S(1)} %pad_maximum_fusion.15), channel_id=1, source_target_pairs={{0,2},{2,4},{4,6},{6,8},{8,10},{10,12},{12,14},{14,0},{1,3},{3,5},... | collective-permute-start | bytes 786440 | tf_op jit(solution)/shard_map/ppermute | solution.py:23
  373.5 22.4 %collective-permute-start.30 = (bf16[64,2048]{1,0:T(8,128)(2,1)S(1)}, bf16[64,2048]{1,0:T(8,128)(2,1)}, u32[]{:S(2)}, u32[]{:S(2)}) collective-permute-start(bf16[64,2048]{1,0:T(8,128)(2,1)S(1)} %pad_maximum_fusion.16), channel_id=1, source_target_pairs={{0,14},{2,0},{4,2},{6,4},{8,6},{10,8},{12,10},{14,12},{1,15},{3,1}... | collective-permute-start | bytes 786440 | tf_op jit(solution)/shard_map/ppermute | solution.py:23
  380.6 15.4 %collective-permute-start.27 = (bf16[64,2048]{1,0:T(8,128)(2,1)S(1)}, bf16[64,2048]{1,0:T(8,128)(2,1)S(1)}, u32[]{:S(2)}, u32[]{:S(2)}) collective-permute-start(bf16[64,2048]{1,0:T(8,128)(2,1)S(1)} %fusion.46), channel_id=1, source_target_pairs={{0,2},{2,4},{4,6},{6,8},{8,10},{10,12},{12,14},{14,0},{1,3},{3,5},... | collective-permute-start | bytes 786440 | tf_op jit(solution)/shard_map/ppermute | solution.py:23
  396.0 19.4 %copy-start.8 = (bf16[64,2048]{1,0:T(8,128)(2,1)S(1)}, bf16[64,2048]{1,0:T(8,128)(2,1)}, u32[]{:S(2)}) copy-start(bf16[64,2048]{1,0:T(8,128)(2,1)} %copy-done.7) | copy-start | bytes 786436
  397.8 9.2 %collective-permute-start.31 = (bf16[64,2048]{1,0:T(8,128)(2,1)S(1)}, bf16[64,2048]{1,0:T(8,128)(2,1)S(1)}, u32[]{:S(2)}, u32[]{:S(2)}) collective-permute-start(bf16[64,2048]{1,0:T(8,128)(2,1)S(1)} %get-tuple-element.44), channel_id=1, source_target_pairs={{0,14},{2,0},{4,2},{6,4},{8,6},{10,8},{12,10},{14,12},{1,15},{3,1}... | collective-permute-start | bytes 786440 | tf_op jit(solution)/shard_map/ppermute | solution.py:23
  397.8 9.3 %collective-permute-start.28 = (bf16[64,2048]{1,0:T(8,128)(2,1)}, bf16[64,2048]{1,0:T(8,128)(2,1)S(1)}, u32[]{:S(2)}, u32[]{:S(2)}) collective-permute-start(bf16[64,2048]{1,0:T(8,128)(2,1)} %get-tuple-element.43), channel_id=1, source_target_pairs={{0,2},{2,4},{4,6},{6,8},{8,10},{10,12},{12,14},{14,0},{1,3},{3,5},... | collective-permute-start | bytes 786440 | tf_op jit(solution)/shard_map/ppermute | solution.py:23
  407.0 8.4 %collective-permute-start.32 = (bf16[64,2048]{1,0:T(8,128)(2,1)S(1)}, bf16[64,2048]{1,0:T(8,128)(2,1)S(1)}, u32[]{:S(2)}, u32[]{:S(2)}) collective-permute-start(bf16[64,2048]{1,0:T(8,128)(2,1)S(1)} %fusion.45), channel_id=1, source_target_pairs={{0,14},{2,0},{4,2},{6,4},{8,6},{10,8},{12,10},{14,12},{1,15},{3,1}... | collective-permute-start | bytes 786440 | tf_op jit(solution)/shard_map/ppermute | solution.py:23
  (11 other events, 18.8 us)
